TPU v7x, 128 devices: a whole 4x4x4 slice. The times are simulated.
128 devices in a mesh: gx: 8 (over x, core), yz: 16 (over z, y).
Axes of the slice: x: 4, y: 4, z: 4, core: 2. Of those that a mesh axis runs over, the one named last changes fastest.
Arguments:
- perm_class: int32 [256, 512, 512], P('gx', 'yz'), may hold values from 0 to 7
- class_drag: float32 [8], replicated, may hold values from 0.05 to 20
- force: float32 [256, 512, 512], P('gx', 'yz'), may hold values from -6 to 6
- coarse_inverse: float32 [128, 128], replicated, may hold values from -0.5 to 0.5
- coarse_owner: int32 [128], replicated, may hold values from 0 to 127, each once
Outputs:
- velocity: float32 [256, 512, 512], P('gx', 'yz')
- mult_x: float32 [8, 512, 512], P('gx', 'yz')
- mult_y: float32 [256, 16, 512], P('gx', 'yz')
Inputs may be any that keep to these rules, and one draw needn't show every extreme that they name: coarse_owner is a permutation: each coarse row belongs to exactly one subdomain.
All inputs are finite; a program needn't handle non-finite values.
Results may differ from a plain program's by a relative error of at most 0.0001.
Values sent between devices are 32-bit elements; how exact they have to be, the bound alone decides.
A program may use at most 128 MiB of HBM per device.

v0:
```python
import jax
import jax.numpy as jnp
from jax import lax
from jax.sharding import PartitionSpec as P

CLASSES = 8
SWEEPS = 8
ITERS = 2


def extended(x, sides, width):
    for axis, dim in sides:
        devices, length = (lax.axis_size(axis), x.shape[dim])
        up = [(i, (i + 1) % devices) for i in range(devices - 1)]
        down = [(j, i) for i, j in up]
        last = lax.slice_in_dim(x, length - width, length, axis=dim)
        initial = lax.slice_in_dim(x, 0, width, axis=dim)
        before = lax.ppermute(last, axis, up)
        after = lax.ppermute(initial, axis, down)
        x = jnp.concatenate([before, x, after], axis=dim)
    return x


def operate(field, drag_field):
    padded = jnp.pad(field, 1)
    beside = padded[2:, 1:-1, 1:-1] + padded[:-2, 1:-1, 1:-1]
    beside = beside + padded[1:-1, 2:, 1:-1] + padded[1:-1, :-2, 1:-1]
    beside = beside + padded[1:-1, 1:-1, 2:] + padded[1:-1, 1:-1, :-2]
    return (6.0 + drag_field) * field - beside


def inner_solve(right_side, start_field, drag_field):
    solution = start_field
    residual = right_side - operate(solution, drag_field)
    direction = residual
    norm_now = jnp.sum(residual * residual)
    for sweep_index in range(SWEEPS):
        image = operate(direction, drag_field)
        alpha = norm_now / jnp.sum(direction * image)
        solution = solution + alpha * direction
        residual = residual - alpha * image
        norm_next = jnp.sum(residual * residual)
        direction = residual + norm_next / norm_now * direction
        norm_now = norm_next
    return solution


def spread(weights, values):
    return weights[:, :, None] * values[None, None, :]


def on_device(perm_class, class_drag, force, coarse_inverse, coarse_owner):
    width_x, width_y, depth = force.shape
    count_x = lax.axis_size("gx")
    count_y = lax.axis_size("yz")
    index_x = lax.axis_index("gx")
    index_y = lax.axis_index("yz")
    device_id = index_x * count_y + index_y
    drag_field = jnp.zeros(force.shape, jnp.float32)
    for level in range(CLASSES):
        drag_field = drag_field + jnp.where(perm_class == level, class_drag[level], 0.0)
    owner_self = coarse_owner[device_id]
    has_right = (index_x < count_x - 1).astype(jnp.float32)
    has_left = (index_x > 0).astype(jnp.float32)
    has_upper = (index_y < count_y - 1).astype(jnp.float32)
    has_lower = (index_y > 0).astype(jnp.float32)
    lam_hi_x = jnp.zeros((width_y, depth), jnp.float32)
    lam_lo_x = jnp.zeros((width_y, depth), jnp.float32)
    lam_hi_y = jnp.zeros((width_x, depth), jnp.float32)
    lam_lo_y = jnp.zeros((width_x, depth), jnp.float32)
    solution = jnp.zeros(force.shape, jnp.float32)
    wide_x = jnp.arange(width_x, dtype=jnp.float32) / (width_x - 1)
    wide_y = jnp.arange(width_y, dtype=jnp.float32) / (width_y - 1)
    area_a = (1.0 - wide_x)[:, None] * (1.0 - wide_y)[None, :]
    area_b = (1.0 - wide_x)[:, None] * wide_y[None, :]
    area_c = wide_x[:, None] * (1.0 - wide_y)[None, :]
    area_d = wide_x[:, None] * wide_y[None, :]
    total_if = float(
        (count_x - 1) * count_y * width_y * depth + count_x * width_x * (count_y - 1) * depth
    )
    row_weights = coarse_inverse[owner_self][coarse_owner]
    for outer_index in range(ITERS):
        load = jnp.zeros(force.shape, jnp.float32)
        load = load.at[width_x - 1].add(-lam_hi_x)
        load = load.at[0].add(lam_lo_x)
        load = load.at[:, width_y - 1].add(-lam_hi_y)
        load = load.at[:, 0].add(lam_lo_y)
        solution = inner_solve(force + load, solution, drag_field)
        corners = jnp.stack([solution[0, 0], solution[0, -1], solution[-1, 0], solution[-1, -1]])[
            None
        ]
        correction = jnp.einsum(
            "t,tcz->cz",
            row_weights,
            lax.all_gather(corners, ("gx", "yz"), axis=0, tiled=True),
            precision=lax.Precision.HIGHEST,
        )
        added = spread(area_a, correction[0]) + spread(area_b, correction[1])
        added = added + spread(area_c, correction[2])
        added = added + spread(area_d, correction[3])
        solution = solution + added
        padded = extended(solution, (("gx", 0), ("yz", 1)), 1)
        right_layer = padded[-1, 1:-1]
        left_layer = padded[0, 1:-1]
        upper_layer = padded[1:-1, -1]
        lower_layer = padded[1:-1, 0]
        jump_hi_x = (solution[-1] - right_layer) * has_right
        jump_lo_x = (left_layer - solution[0]) * has_left
        jump_hi_y = (solution[:, -1] - upper_layer) * has_upper
        jump_lo_y = (lower_layer - solution[:, 0]) * has_lower
        local_total = jnp.sum(jump_hi_x * jump_hi_x) + jnp.sum(jump_hi_y * jump_hi_y)
        total = lax.psum(local_total, ("gx", "yz"))
        step_size = 0.5 / jnp.sqrt(total / total_if + 1e-06)
        lam_hi_x = lam_hi_x + step_size * jump_hi_x
        lam_lo_x = lam_lo_x + step_size * jump_lo_x
        lam_hi_y = lam_hi_y + step_size * jump_hi_y
        lam_lo_y = lam_lo_y + step_size * jump_lo_y
    return (solution, lam_hi_x[None], lam_hi_y[:, None])


def solution(mesh):
    return jax.shard_map(
        on_device,
        mesh=mesh,
        in_specs=(P("gx", "yz", None), P(), P("gx", "yz", None), P(), P()),
        out_specs=(P("gx", "yz", None), P("gx", "yz", None), P("gx", "yz", None)),
        check_vma=False,
    )
```

profile of v0, /device:TPU:1, one launch (start us, length us, event | category | flops | bytes accessed | tf_op | source)
XLA Modules:
  0.0 725.6 jit_solution(8997574419479634911)
XLA Ops:
  9.1 12.7 %fusion.111 = f32[32,32,512]{2,0,1:T(8,128)S(1)} fusion(f32[32,32,512]{2,0,1:T(8,128)S(1)} %broadcast.307, f32[32,32,512]{2,0,1:T(8,128)} %constant.227.clone.1, f32[32,32,512]{2,1,0:T(8,128)} %param.23, f32[]{:T(128)} %bitcast.7, f32[]{:T(128)} %bitcast.6, f32[]{:T(128)} %bitcast.5, f32[]{:T(128)} %bitcast.4, f32[]{:T(128)} %bitcast.3, f32[]{:T(128)} %bitcast.2, ...), kind=kLoop, calls=%fused_computation.220 | loop fusion | flops 17301504 | bytes 10485792 | tf_op jit(solution)/shard_map/sub | solution.py:34
  21.8 11.4 %multiply_reduce_fusion.28 = (f32[]{:T(128)}, f32[]{:T(128)}, f32[32,32,512]{2,0,1:T(8,128)}) fusion(f32[32,32,512]{2,0,1:T(8,128)S(1)} %fusion.111, f32[]{:T(128)} %bitcast.7, f32[]{:T(128)} %bitcast.6, f32[]{:T(128)} %bitcast.5, f32[]{:T(128)} %bitcast.4, f32[]{:T(128)} %bitcast.3, f32[]{:T(128)} %bitcast.2, f32[]{:T(128)} %bitcast.1, f32[]{:T(128)} %bitcast, ...), kind=kLoop, calls=%fused_computation.281 | loop fusion | flops 18350080 | bytes 6291496 | tf_op jit(solution)/shard_map/reduce_sum | solution.py:39
  34.5 4.9 multiply_reduce_fusion.27
  43.4 11.0 %multiply_reduce_fusion.26 = (f32[]{:T(128)}, f32[32,32,512]{2,0,1:T(8,128)}) fusion(f32[32,32,512]{2,0,1:T(8,128)S(1)} %multiply_add_fusion.15, f32[]{:T(128)} %bitcast.7, f32[]{:T(128)} %bitcast.6, f32[]{:T(128)} %bitcast.5, f32[]{:T(128)} %bitcast.4, f32[]{:T(128)} %bitcast.3, f32[]{:T(128)} %bitcast.2, f32[]{:T(128)} %bitcast.1, f32[]{:T(128)} %bitcast, ...), kind=kLoop, calls=%fused_computation.277 | loop fusion | flops 17301504 | bytes 6291492 | tf_op jit(solution)/shard_map/reduce_sum | solution.py:39
  60.5 3.6 multiply_add_fusion.14
  64.1 11.3 %multiply_reduce_fusion.24 = (f32[]{:T(128)}, f32[32,32,512]{2,0,1:T(8,128)}) fusion(f32[32,32,512]{2,0,1:T(8,128)S(1)} %multiply_add_fusion.14, f32[]{:T(128)} %bitcast.7, f32[]{:T(128)} %bitcast.6, f32[]{:T(128)} %bitcast.5, f32[]{:T(128)} %bitcast.4, f32[]{:T(128)} %bitcast.3, f32[]{:T(128)} %bitcast.2, f32[]{:T(128)} %bitcast.1, f32[]{:T(128)} %bitcast, ...), kind=kLoop, calls=%fused_computation.273 | loop fusion | flops 17301504 | bytes 6291492 | tf_op jit(solution)/shard_map/reduce_sum | solution.py:39
  76.7 5.8 multiply_reduce_fusion.23
  86.5 11.0 %multiply_reduce_fusion.22 = (f32[]{:T(128)}, f32[32,32,512]{2,0,1:T(8,128)}) fusion(f32[32,32,512]{2,0,1:T(8,128)S(1)} %multiply_add_fusion.13, f32[]{:T(128)} %bitcast.7, f32[]{:T(128)} %bitcast.6, f32[]{:T(128)} %bitcast.5, f32[]{:T(128)} %bitcast.4, f32[]{:T(128)} %bitcast.3, f32[]{:T(128)} %bitcast.2, f32[]{:T(128)} %bitcast.1, f32[]{:T(128)} %bitcast, ...), kind=kLoop, calls=%fused_computation.269 | loop fusion | flops 17301504 | bytes 6291492 | tf_op jit(solution)/shard_map/reduce_sum | solution.py:39
  103.5 3.6 multiply_add_fusion.12
  107.1 11.1 %multiply_reduce_fusion.20 = (f32[]{:T(128)}, f32[32,32,512]{2,0,1:T(8,128)}) fusion(f32[32,32,512]{2,0,1:T(8,128)S(1)} %multiply_add_fusion.12, f32[]{:T(128)} %bitcast.7, f32[]{:T(128)} %bitcast.6, f32[]{:T(128)} %bitcast.5, f32[]{:T(128)} %bitcast.4, f32[]{:T(128)} %bitcast.3, f32[]{:T(128)} %bitcast.2, f32[]{:T(128)} %bitcast.1, f32[]{:T(128)} %bitcast, ...), kind=kLoop, calls=%fused_computation.265 | loop fusion | flops 17301504 | bytes 6291492 | tf_op jit(solution)/shard_map/reduce_sum | solution.py:39
  119.4 5.9 multiply_reduce_fusion.19
  129.3 22.1 %multiply_reduce_fusion.18 = (f32[]{:T(128)}, f32[32,32,512]{2,0,1:T(8,128)}) fusion(f32[32,32,512]{2,0,1:T(8,128)S(1)} %multiply_add_fusion.11, f32[]{:T(128)} %bitcast.7, f32[]{:T(128)} %bitcast.6, f32[]{:T(128)} %bitcast.5, f32[]{:T(128)} %bitcast.4, f32[]{:T(128)} %bitcast.3, f32[]{:T(128)} %bitcast.2, f32[]{:T(128)} %bitcast.1, f32[]{:T(128)} %bitcast, ...), kind=kLoop, calls=%fused_computation.261 | loop fusion | flops 17301504 | bytes 6291492 | tf_op jit(solution)/shard_map/reduce_sum | solution.py:39
  152.8 3.4 multiply_reduce_fusion.17
  157.5 3.6 multiply_add_fusion.10
  161.1 11.1 %multiply_reduce_fusion.16 = (f32[]{:T(128)}, f32[32,32,512]{2,0,1:T(8,128)}) fusion(f32[32,32,512]{2,0,1:T(8,128)S(1)} %multiply_add_fusion.10, f32[]{:T(128)} %bitcast.7, f32[]{:T(128)} %bitcast.6, f32[]{:T(128)} %bitcast.5, f32[]{:T(128)} %bitcast.4, f32[]{:T(128)} %bitcast.3, f32[]{:T(128)} %bitcast.2, f32[]{:T(128)} %bitcast.1, f32[]{:T(128)} %bitcast, ...), kind=kLoop, calls=%fused_computation.257 | loop fusion | flops 17301504 | bytes 6291492 | tf_op jit(solution)/shard_map/reduce_sum | solution.py:39
  173.5 4.2 multiply_reduce_fusion.15
  179.1 4.5 multiply_add_fusion.9
  183.6 10.1 %fusion.113 = f32[]{:T(128)} fusion(f32[32,32,512]{2,0,1:T(8,128)S(1)} %multiply_add_fusion.9, f32[]{:T(128)} %bitcast.7, f32[]{:T(128)} %bitcast.6, f32[]{:T(128)} %bitcast.5, f32[]{:T(128)} %bitcast.4, f32[]{:T(128)} %bitcast.3, f32[]{:T(128)} %bitcast.2, f32[]{:T(128)} %bitcast.1, f32[]{:T(128)} %bitcast, s32[32,32,512]{2,1,0:T(8,128)S(1)} %copy-done.2), kind=kLoop, calls=%fused_computation.285 | loop fusion | flops 17301504 | bytes 4194340 | tf_op jit(solution)/shard_map/reduce_sum | solution.py:39
  195.0 9.7 %multiply_add_fusion.8 = f32[32,32,512]{2,0,1:T(8,128)S(1)} fusion(f32[32,32,512]{2,0,1:T(8,128)} %copy-done.16, f32[32,32,512]{2,0,1:T(8,128)} %copy-done.14, f32[32,32,512]{2,0,1:T(8,128)} %copy-done.12, f32[32,32,512]{2,0,1:T(8,128)} %copy-done.11, f32[32,32,512]{2,0,1:T(8,128)} %copy-done.8, f32[32,32,512]{2,0,1:T(8,128)} %copy-done.7, ...), kind=kLoop, calls=%fused_computation.253 | loop fusion | flops 11010048 | bytes 23068708 | tf_op jit(solution)/shard_map/add | solution.py:40
  210.9 63.1 %all-gather.7.cloned.1.call-done = f32[128,4,512]{2,1,0:T(4,128)} async-done(((f32[1,4,512]{2,1,0:T(4,128)}), f32[128,4,512]{2,1,0:T(4,128)}) %all-gather.7.cloned.1.call-update) | async-done | bytes 1048592 | tf_op jit(solution)/shard_map/all_gather | solution.py:95
  281.7 3.4 collective-permute-done
  292.3 4.6 collective-permute-done.2
  301.5 65.9 %psum.14 = f32[]{:T(128)} all-reduce(f32[]{:T(128)S(6)} %add.626), channel_id=1, replica_groups=mesh['gx'=8,'yz'=16] {'gx','yz'}, use_global_device_ids=true, to_apply=%region_18.19 | all-reduce | flops 1 | bytes 8 | tf_op jit(solution)/shard_map/psum | solution.py:112
  375.9 16.8 %fusion.55 = f32[32,32,512]{2,0,1:T(8,128)S(1)} fusion(f32[32,32,512]{2,0,1:T(8,128)} %copy-done.17, f32[32,32,512]{2,0,1:T(8,128)} %fusion.122, f32[32,32,512]{2,1,0:T(8,128)} %param.23, f32[]{:T(128)} %bitcast.7, f32[]{:T(128)} %bitcast.6, f32[]{:T(128)} %bitcast.5, f32[]{:T(128)} %bitcast.4, f32[]{:T(128)} %bitcast.3, f32[]{:T(128)} %bitcast.2, ...), kind=kLoop, calls=%fused_computation.164 | loop fusion | flops 17301504 | bytes 10485792 | tf_op jit(solution)/shard_map/sub | solution.py:34
  392.8 11.3 %multiply_reduce_fusion.13 = (f32[]{:T(128)}, f32[]{:T(128)}, f32[32,32,512]{2,0,1:T(8,128)}) fusion(f32[32,32,512]{2,0,1:T(8,128)S(1)} %fusion.55, f32[]{:T(128)} %bitcast.7, f32[]{:T(128)} %bitcast.6, f32[]{:T(128)} %bitcast.5, f32[]{:T(128)} %bitcast.4, f32[]{:T(128)} %bitcast.3, f32[]{:T(128)} %bitcast.2, f32[]{:T(128)} %bitcast.1, f32[]{:T(128)} %bitcast, ...), kind=kLoop, calls=%fused_computation.250 | loop fusion | flops 18350080 | bytes 6291496 | tf_op jit(solution)/shard_map/reduce_sum | solution.py:39
  405.4 4.9 multiply_reduce_fusion.12
  414.3 11.0 %multiply_reduce_fusion.11 = (f32[]{:T(128)}, f32[32,32,512]{2,0,1:T(8,128)}) fusion(f32[32,32,512]{2,0,1:T(8,128)S(1)} %multiply_add_fusion.7, f32[]{:T(128)} %bitcast.7, f32[]{:T(128)} %bitcast.6, f32[]{:T(128)} %bitcast.5, f32[]{:T(128)} %bitcast.4, f32[]{:T(128)} %bitcast.3, f32[]{:T(128)} %bitcast.2, f32[]{:T(128)} %bitcast.1, f32[]{:T(128)} %bitcast, ...), kind=kLoop, calls=%fused_computation.246 | loop fusion | flops 17301504 | bytes 6291492 | tf_op jit(solution)/shard_map/reduce_sum | solution.py:39
  426.6 3.4 multiply_reduce_fusion.10
  431.4 3.6 multiply_add_fusion.6
  435.1 11.2 %multiply_reduce_fusion.9 = (f32[]{:T(128)}, f32[32,32,512]{2,0,1:T(8,128)}) fusion(f32[32,32,512]{2,0,1:T(8,128)S(1)} %multiply_add_fusion.6, f32[]{:T(128)} %bitcast.7, f32[]{:T(128)} %bitcast.6, f32[]{:T(128)} %bitcast.5, f32[]{:T(128)} %bitcast.4, f32[]{:T(128)} %bitcast.3, f32[]{:T(128)} %bitcast.2, f32[]{:T(128)} %bitcast.1, f32[]{:T(128)} %bitcast, ...), kind=kLoop, calls=%fused_computation.242 | loop fusion | flops 17301504 | bytes 6291492 | tf_op jit(solution)/shard_map/reduce_sum | solution.py:39
  447.6 5.9 multiply_reduce_fusion.8
  457.5 11.0 %multiply_reduce_fusion.7 = (f32[]{:T(128)}, f32[32,32,512]{2,0,1:T(8,128)}) fusion(f32[32,32,512]{2,0,1:T(8,128)S(1)} %multiply_add_fusion.5, f32[]{:T(128)} %bitcast.7, f32[]{:T(128)} %bitcast.6, f32[]{:T(128)} %bitcast.5, f32[]{:T(128)} %bitcast.4, f32[]{:T(128)} %bitcast.3, f32[]{:T(128)} %bitcast.2, f32[]{:T(128)} %bitcast.1, f32[]{:T(128)} %bitcast, ...), kind=kLoop, calls=%fused_computation.238 | loop fusion | flops 17301504 | bytes 6291492 | tf_op jit(solution)/shard_map/reduce_sum | solution.py:39
  469.8 3.4 multiply_reduce_fusion.6
  474.5 3.6 multiply_add_fusion.4
  478.2 11.1 %multiply_reduce_fusion.5 = (f32[]{:T(128)}, f32[32,32,512]{2,0,1:T(8,128)}) fusion(f32[32,32,512]{2,0,1:T(8,128)S(1)} %multiply_add_fusion.4, f32[]{:T(128)} %bitcast.7, f32[]{:T(128)} %bitcast.6, f32[]{:T(128)} %bitcast.5, f32[]{:T(128)} %bitcast.4, f32[]{:T(128)} %bitcast.3, f32[]{:T(128)} %bitcast.2, f32[]{:T(128)} %bitcast.1, f32[]{:T(128)} %bitcast, ...), kind=kLoop, calls=%fused_computation.234 | loop fusion | flops 17301504 | bytes 6291492 | tf_op jit(solution)/shard_map/reduce_sum | solution.py:39
  490.6 5.8 multiply_reduce_fusion.4
  500.4 11.3 %multiply_reduce_fusion.3 = (f32[]{:T(128)}, f32[32,32,512]{2,0,1:T(8,128)}) fusion(f32[32,32,512]{2,0,1:T(8,128)S(1)} %multiply_add_fusion.3, f32[]{:T(128)} %bitcast.7, f32[]{:T(128)} %bitcast.6, f32[]{:T(128)} %bitcast.5, f32[]{:T(128)} %bitcast.4, f32[]{:T(128)} %bitcast.3, f32[]{:T(128)} %bitcast.2, f32[]{:T(128)} %bitcast.1, f32[]{:T(128)} %bitcast, ...), kind=kLoop, calls=%fused_computation.230 | loop fusion | flops 17301504 | bytes 6291492 | tf_op jit(solution)/shard_map/reduce_sum | solution.py:39
  512.9 3.4 multiply_reduce_fusion.2
  517.6 3.6 multiply_add_fusion.2
  521.3 11.0 %multiply_reduce_fusion.1 = (f32[]{:T(128)}, f32[32,32,512]{2,0,1:T(8,128)}) fusion(f32[32,32,512]{2,0,1:T(8,128)S(1)} %multiply_add_fusion.2, f32[]{:T(128)} %bitcast.7, f32[]{:T(128)} %bitcast.6, f32[]{:T(128)} %bitcast.5, f32[]{:T(128)} %bitcast.4, f32[]{:T(128)} %bitcast.3, f32[]{:T(128)} %bitcast.2, f32[]{:T(128)} %bitcast.1, f32[]{:T(128)} %bitcast, ...), kind=kLoop, calls=%fused_computation.226 | loop fusion | flops 17301504 | bytes 6291492 | tf_op jit(solution)/shard_map/reduce_sum | solution.py:39
  533.6 4.2 multiply_reduce_fusion
  539.1 4.5 multiply_add_fusion.1
  543.7 10.1 %fusion.112 = f32[]{:T(128)} fusion(f32[32,32,512]{2,0,1:T(8,128)S(1)} %multiply_add_fusion.1, f32[]{:T(128)} %bitcast.7, f32[]{:T(128)} %bitcast.6, f32[]{:T(128)} %bitcast.5, f32[]{:T(128)} %bitcast.4, f32[]{:T(128)} %bitcast.3, f32[]{:T(128)} %bitcast.2, f32[]{:T(128)} %bitcast.1, f32[]{:T(128)} %bitcast, s32[32,32,512]{2,1,0:T(8,128)S(1)} %copy-done.2), kind=kLoop, calls=%fused_computation.284 | loop fusion | flops 17301504 | bytes 4194340 | tf_op jit(solution)/shard_map/reduce_sum | solution.py:39
  555.1 9.2 %multiply_add_fusion = f32[32,32,512]{2,0,1:T(8,128)S(1)} fusion(f32[32,32,512]{2,0,1:T(8,128)} %copy-done.15, f32[32,32,512]{2,0,1:T(8,128)} %copy-done.13, f32[32,32,512]{2,0,1:T(8,128)} %copy-done.10, f32[32,32,512]{2,0,1:T(8,128)} %copy-done.9, f32[32,32,512]{2,0,1:T(8,128)} %copy-done.6, f32[32,32,512]{2,0,1:T(8,128)} %copy-done.5, ...), kind=kLoop, calls=%fused_computation.222 | loop fusion | flops 15728640 | bytes 25190436 | tf_op jit(solution)/shard_map/add | solution.py:40
  565.0 61.5 %all-gather.9.cloned.1.call-done = f32[128,4,512]{2,1,0:T(4,128)} async-done(((f32[1,4,512]{2,1,0:T(4,128)}), f32[128,4,512]{2,1,0:T(4,128)}) %all-gather.9.cloned.1.call-update) | async-done | bytes 1048592 | tf_op jit(solution)/shard_map/all_gather | solution.py:95
  632.7 3.4 collective-permute-done.4
  641.4 4.6 collective-permute-done.6
  650.5 65.6 %psum.15 = f32[]{:T(128)} all-reduce(f32[]{:T(128)S(6)} %add.695), channel_id=1, replica_groups=mesh['gx'=8,'yz'=16] {'gx','yz'}, use_global_device_ids=true, to_apply=%region_37.38 | all-reduce | flops 1 | bytes 8 | tf_op jit(solution)/shard_map/psum | solution.py:112
  (104 shorter events, 71.9 us)
Async XLA Ops:
  7.2 202.3 %copy-start = (f32[128,128]{1,0:T(8,128)S(1)}, f32[128,128]{1,0:T(8,128)}, u32[]{:S(2)}) copy-start(f32[128,128]{1,0:T(8,128)} %param.24) | copy-start | bytes 196612
  7.2 1.9 copy-start.2
  7.2 266.8 %all-gather.7.cloned.1.call-start = ((), (), s32[]{:S(2)}) async-start(), calls=%async_computation | async-start | bytes 1056768 | tf_op jit(solution)/shard_map/all_gather | solution.py:95
  21.8 11.4 %copy-start.4 = (f32[32,32,512]{2,0,1:T(8,128)}, f32[32,32,512]{2,0,1:T(8,128)S(1)}, u32[]{:S(2)}) copy-start(f32[32,32,512]{2,0,1:T(8,128)S(1)} %fusion.111) | copy-start | bytes 6291460
  43.4 11.1 %copy-start.7 = (f32[32,32,512]{2,0,1:T(8,128)}, f32[32,32,512]{2,0,1:T(8,128)S(1)}, u32[]{:S(2)}) copy-start(f32[32,32,512]{2,0,1:T(8,128)S(1)} %multiply_add_fusion.15) | copy-start | bytes 6291460
  64.1 11.3 %copy-start.8 = (f32[32,32,512]{2,0,1:T(8,128)}, f32[32,32,512]{2,0,1:T(8,128)S(1)}, u32[]{:S(2)}) copy-start(f32[32,32,512]{2,0,1:T(8,128)S(1)} %multiply_add_fusion.14) | copy-start | bytes 6291460
  86.5 11.0 %copy-start.11 = (f32[32,32,512]{2,0,1:T(8,128)}, f32[32,32,512]{2,0,1:T(8,128)S(1)}, u32[]{:S(2)}) copy-start(f32[32,32,512]{2,0,1:T(8,128)S(1)} %multiply_add_fusion.13) | copy-start | bytes 6291460
  107.1 11.1 %copy-start.12 = (f32[32,32,512]{2,0,1:T(8,128)}, f32[32,32,512]{2,0,1:T(8,128)S(1)}, u32[]{:S(2)}) copy-start(f32[32,32,512]{2,0,1:T(8,128)S(1)} %multiply_add_fusion.12) | copy-start | bytes 6291460
  129.3 22.2 %copy-start.14 = (f32[32,32,512]{2,0,1:T(8,128)}, f32[32,32,512]{2,0,1:T(8,128)S(1)}, u32[]{:S(2)}) copy-start(f32[32,32,512]{2,0,1:T(8,128)S(1)} %multiply_add_fusion.11) | copy-start | bytes 6291460
  161.1 11.1 %copy-start.16 = (f32[32,32,512]{2,0,1:T(8,128)}, f32[32,32,512]{2,0,1:T(8,128)S(1)}, u32[]{:S(2)}) copy-start(f32[32,32,512]{2,0,1:T(8,128)S(1)} %multiply_add_fusion.10) | copy-start | bytes 6291460
  195.0 11.8 %copy-start.20 = (s32[128]{0:T(128)S(1)}, s32[128]{0:T(128)}, u32[]{:S(2)}) copy-start(s32[128]{0:T(128)} %param.25) | copy-start | bytes 1540
  204.7 1.3 copy-start.18
  206.7 419.7 %all-gather.9.cloned.1.call-start = ((), (), s32[]{:S(2)}) async-start(), calls=%async_computation.1 | async-start | bytes 1056768 | tf_op jit(solution)/shard_map/all_gather | solution.py:95
  278.1 1.4 copy-start.17
  279.5 5.6 collective-permute-start
  286.9 3.2 collective-permute-start.1
  291.0 5.9 collective-permute-start.2
  299.6 74.8 %collective-permute-start.3 = (f32[34,1,512]{2,0,1:T(8,128)S(1)}, f32[34,1,512]{2,0,1:T(8,128)S(1)}, u32[]{:S(2)}, u32[]{:S(2)}) collective-permute-start(f32[34,1,512]{2,0,1:T(8,128)S(1)} %get-tuple-element.148), channel_id=1, source_target_pairs={{0,1},{1,2},{2,3},{3,4},{4,5},{5,6},{6,7},{7,8},{8,9},{9,10},{10,1... | collective-permute-start | bytes 208904 | tf_op jit(solution)/shard_map/ppermute | solution.py:18
  392.7 11.3 %copy-start.3 = (f32[32,32,512]{2,0,1:T(8,128)}, f32[32,32,512]{2,0,1:T(8,128)S(1)}, u32[]{:S(2)}) copy-start(f32[32,32,512]{2,0,1:T(8,128)S(1)} %fusion.55) | copy-start | bytes 6291460
  414.3 11.1 %copy-start.5 = (f32[32,32,512]{2,0,1:T(8,128)}, f32[32,32,512]{2,0,1:T(8,128)S(1)}, u32[]{:S(2)}) copy-start(f32[32,32,512]{2,0,1:T(8,128)S(1)} %multiply_add_fusion.7) | copy-start | bytes 6291460
  435.0 11.2 %copy-start.6 = (f32[32,32,512]{2,0,1:T(8,128)}, f32[32,32,512]{2,0,1:T(8,128)S(1)}, u32[]{:S(2)}) copy-start(f32[32,32,512]{2,0,1:T(8,128)S(1)} %multiply_add_fusion.6) | copy-start | bytes 6291460
  457.5 11.0 %copy-start.9 = (f32[32,32,512]{2,0,1:T(8,128)}, f32[32,32,512]{2,0,1:T(8,128)S(1)}, u32[]{:S(2)}) copy-start(f32[32,32,512]{2,0,1:T(8,128)S(1)} %multiply_add_fusion.5) | copy-start | bytes 6291460
  478.1 11.1 %copy-start.10 = (f32[32,32,512]{2,0,1:T(8,128)}, f32[32,32,512]{2,0,1:T(8,128)S(1)}, u32[]{:S(2)}) copy-start(f32[32,32,512]{2,0,1:T(8,128)S(1)} %multiply_add_fusion.4) | copy-start | bytes 6291460
  500.4 11.3 %copy-start.13 = (f32[32,32,512]{2,0,1:T(8,128)}, f32[32,32,512]{2,0,1:T(8,128)S(1)}, u32[]{:S(2)}) copy-start(f32[32,32,512]{2,0,1:T(8,128)S(1)} %multiply_add_fusion.3) | copy-start | bytes 6291460
  521.2 11.1 %copy-start.15 = (f32[32,32,512]{2,0,1:T(8,128)}, f32[32,32,512]{2,0,1:T(8,128)S(1)}, u32[]{:S(2)}) copy-start(f32[32,32,512]{2,0,1:T(8,128)S(1)} %multiply_add_fusion.2) | copy-start | bytes 6291460
  564.2 64.3 %copy-start.19 = (f32[32,32,512]{2,0,1:T(8,128)}, f32[32,32,512]{2,0,1:T(8,128)S(1)}, u32[]{:S(2)}) copy-start(f32[32,32,512]{2,0,1:T(8,128)S(1)} %multiply_add_fusion) | copy-start | bytes 6291460
  630.6 5.6 collective-permute-start.4
  636.9 3.2 collective-permute-start.5
  640.1 5.9 collective-permute-start.6
  646.6 71.7 %copy-start.1 = (f32[128,128]{1,0:T(8,128)S(1)}, f32[128,128]{1,0:T(8,128)}, u32[]{:S(2)}) copy-start(f32[128,128]{1,0:T(8,128)} %param.24) | copy-start | bytes 196612
Sparse Core Ops, SparseCore 0:
  206.8 67.1 all-gather.6
  565.1 61.2 all-gather.8
where the time goes:
time: 736 us; the launch traced here: 726 us
  other arithmetic  360 us (49%)
  waiting for transfers between devices  143 us (19%)
  blocking collectives  132 us (18%)
  between operations  59.9 us (8%)
  local copies, waits for them, and re-layouts  14.2 us (2%)
  starting transfers between devices  12.6 us (2%)
    reduce_sum x16, other arithmetic, inner_solve(): alpha = norm_now / jnp.sum(direction * image)  187 us
    psum x2, blocking collectives, on_device(): total = lax.psum(local_total, ('gx', 'yz'))  132 us
    all_gather x2, waiting for transfers between devices, on_device(): lax.all_gather(corners, ('gx', 'yz'), axis=0, tiled=True)  125 us
    reduce_sum x14, other arithmetic, inner_solve(): norm_next = jnp.sum(residual * residual)  62 us
    add x14, other arithmetic, inner_solve(): direction = residual + norm_next / norm_now * direction  47.1 us
    sub x2, other arithmetic, inner_solve(): residual = right_side - operate(solution, drag_field)  29.5 us
    add x2, other arithmetic, inner_solve(): solution = solution + alpha * direction  18.9 us
    ppermute x4, waiting for transfers between devices, extended(): after = lax.ppermute(initial, axis, down)  16 us
  transfers between devices with their start and end apart: 9, of which 8 were waited for; matrix products, arithmetic and copies ran while one was open for 1% of the time, Pallas kernels for 0%

commit v1 on v0

v1 whole, which is shorter than its diff:
```python
import functools

import jax
import jax.numpy as jnp
from jax import lax
from jax.experimental import pallas as pl
from jax.experimental.pallas import tpu as pltpu
from jax.sharding import PartitionSpec as P

CLASSES = 8
SWEEPS = 8
ITERS = 2
F32 = jnp.float32
MESH = pl.DeviceIdType.MESH
PLANE = 128
UNROLL = 8


def rows(x):
    return pl.ds(pl.multiple_of(x * PLANE, PLANE), PLANE)


def tiles(value):
    return value.reshape(4, 4, 8, 128)


def beside_yz(cur):
    lane = lax.broadcasted_iota(jnp.int32, (4, 4, 8, 128), 3)
    sub = lax.broadcasted_iota(jnp.int32, (4, 1, 8, 128), 2)
    gap = jnp.zeros((1, 4, 8, 128), F32)
    up = pltpu.roll(cur, 1, 3)
    down = pltpu.roll(cur, 127, 3)
    left = jnp.where(lane == 0, jnp.concatenate([gap, up[:-1]], axis=0), up)
    right = jnp.where(lane == 127, jnp.concatenate([down[1:], gap], axis=0), down)
    before = jnp.where(sub == 0, 0.0, pltpu.roll(cur[:, 3:4], 1, 2))
    after = jnp.where(sub == 7, 0.0, pltpu.roll(cur[:, 0:1], 7, 2))
    low = jnp.concatenate([before, cur[:, 0:3]], axis=1)
    high = jnp.concatenate([cur[:, 1:4], after], axis=1)
    return (high + low) + (left + right)


def total_of(a):
    a = jnp.sum(jnp.sum(a, axis=0, keepdims=True), axis=1, keepdims=True)
    return jnp.broadcast_to(a, (8, 128))


def splat(a):
    return a[None, None]


def sweep_pass(k, first, a, b, U, W):
    def fresh(x):
        u = tiles(W[rows(x), :]) - splat(a) * tiles(U[k, rows(x), :])
        u = u - splat(b) * tiles(U[k - 1, rows(x), :])
        U[k + 1, rows(x), :] = u.reshape(PLANE, 128)
        return u

    def step(x, acc):
        uu, uw = acc
        if first:
            above = tiles(U[k + 1, rows(x + 2), :])
        else:
            above = fresh(x + 2)
        cur = tiles(U[k + 1, rows(x + 1), :])
        below = tiles(U[k + 1, rows(x), :])
        w = tiles(U[0, rows(x + 1), :]) * cur - ((above + below) + beside_yz(cur))
        W[rows(x + 1), :] = w.reshape(PLANE, 128)
        return uu + jnp.sum(cur * cur, axis=(0, 1)), uw + jnp.sum(cur * w, axis=(0, 1))

    if not first:
        fresh(1)
    zero = jnp.zeros((8, 128), F32)
    uu, uw = lax.fori_loop(0, 32, step, (zero, zero), unroll=UNROLL)
    g = total_of(uu)
    return g, total_of(uw) / g


def y_weights(width):
    t = lax.broadcasted_iota(jnp.int32, (1, 4, 8, 128), 1)
    s = lax.broadcasted_iota(jnp.int32, (1, 4, 8, 128), 2)
    return (4 * s + t).astype(F32) / (width - 1)


def kernel(
    ni, nj, perm, drag, force, cinv, owner,
    xpre, corr_out, lamx_out, lamy_out,
    U, W, X, fst, pst, cf, wsp, cinv_s, cbuf, G, PB, R, FS, FR, CS, CR, TS, T1, T2, LAM, JMP,
    in_sem, ci_sem, out_sem, sg, rg, sr, rr, sf, rf, sc, rc, s1, r1, s2, r2,
):
    i = lax.axis_index("gx")
    j = lax.axis_index("yz")
    zero = jnp.zeros((8, 128), F32)
    plane0 = jnp.zeros((PLANE, 128), F32)

    barrier = pltpu.get_barrier_semaphore()
    for d in range(1, ni):
        pl.semaphore_signal(barrier, inc=1, device_id={"gx": lax.rem(i + d, ni)}, device_id_type=MESH)
    for d in range(1, nj):
        pl.semaphore_signal(barrier, inc=1, device_id={"yz": lax.rem(j + d, nj)}, device_id_type=MESH)

    loads = []
    for c in range(4):
        cols = pl.ds(c * 128, 128)
        loads.append((
            pltpu.make_async_copy(perm.at[:, cols], pst.at[c], in_sem.at[2 * c]),
            pltpu.make_async_copy(force.at[:, cols], fst.at[c], in_sem.at[2 * c + 1]),
        ))
        for copy in loads[-1]:
            copy.start()
    weights_copy = pltpu.make_async_copy(cinv, cinv_s, ci_sem)
    weights_copy.start()

    for k in range(SWEEPS + 2):
        U[k, rows(0), :] = plane0
        U[k, rows(33), :] = plane0
    W[rows(33), :] = plane0

    level = [6.0 + drag[c] for c in range(CLASSES)]
    for c in range(4):
        for copy in loads[c]:
            copy.wait()

        def stage(x, carry, c=c):
            base = pl.multiple_of(x * 32, 32)
            for t in range(4):
                cls = pst[c, pl.ds(base + t, 8, stride=4), :]
                b0, b1, b2 = (cls & 1) != 0, (cls & 2) != 0, (cls & 4) != 0
                pairs = [jnp.where(b0, level[n + 1], level[n]) for n in range(0, 8, 2)]
                quads = [jnp.where(b1, pairs[1], pairs[0]), jnp.where(b1, pairs[3], pairs[2])]
                at = pl.ds(pl.multiple_of((x + 1) * PLANE + c * 32 + t * 8, 8), 8)
                U[0, at, :] = jnp.where(b2, quads[1], quads[0])
                U[1, at, :] = fst[c, pl.ds(base + t, 8, stride=4), :]
            return carry

        lax.fori_loop(0, 32, stage, 0, unroll=4)

    weights_copy.wait()
    for sx in range(ni):
        row = owner[sx * nj + j]

        def fill(ty, carry, sx=sx, row=row):
            wsp[sx, ty] = jnp.full((8, 128), cinv_s[row, owner[i * nj + ty]], F32)
            return carry

        lax.fori_loop(0, nj, fill, 0, unroll=4)

    has_right = (i < ni - 1).astype(F32)
    has_left = (i > 0).astype(F32)
    has_upper = (j < nj - 1).astype(F32)
    has_lower = (j > 0).astype(F32)
    wy = y_weights(32)
    wx8 = lax.broadcasted_iota(jnp.int32, (32, 128), 0).astype(F32) / 31.0
    right, left = {"gx": lax.rem(i + 1, ni)}, {"gx": lax.rem(i + ni - 1, ni)}
    upper, lower = {"yz": lax.rem(j + 1, nj)}, {"yz": lax.rem(j + nj - 1, nj)}
    sends = []

    def remote(src, dst, ssem, rsem, dev):
        return pltpu.make_async_remote_copy(
            src_ref=src, dst_ref=dst, send_sem=ssem, recv_sem=rsem, device_id=dev, device_id_type=MESH
        )

    for it in range(ITERS):
        g, a = sweep_pass(0, True, zero, zero, U, W)
        cf[0], cf[8] = a, zero

        def body(k, carry):
            g, a, b = carry
            gn, an = sweep_pass(k, False, a, b, U, W)
            bn = gn / g
            cf[k] = an
            cf[8 + k] = bn
            return gn, an, bn

        g, a, b = lax.fori_loop(1, SWEEPS, body, (g, a, zero))

        av = [cf[k] for k in range(SWEEPS)]
        bv = [cf[8 + k] for k in range(SWEEPS)]
        inv, z = [1.0 / av[0]], [jnp.ones((8, 128), F32)]
        for k in range(1, SWEEPS):
            z.append(-z[k - 1] * inv[k - 1])
            inv.append(1.0 / (av[k] - bv[k] * inv[k - 1]))
        y = [None] * SWEEPS
        y[SWEEPS - 1] = z[SWEEPS - 1] * inv[SWEEPS - 1]
        for k in range(SWEEPS - 2, -1, -1):
            y[k] = (z[k] - bv[k + 1] * y[k + 1]) * inv[k]

        for n, x in ((0, 0), (1, 31)):
            f = None if it == 0 else tiles(X[rows(x), :])
            for k in range(SWEEPS):
                term = splat(y[k]) * tiles(U[k + 1, rows(x + 1), :])
                f = term if f is None else f + term
            FS[it, n] = f.reshape(PLANE, 128)
            for m, (t, s) in enumerate(((0, 0), (3, 7))):
                for c in range(4):
                    cbuf[it, pl.ds((2 * n + m) * 4 + c, 1), :] = f[c, t, s : s + 1, :]
        G[it, j] = cbuf[it]
        if it == 0:
            pl.semaphore_wait(barrier, ni + nj - 2)
        gather = []
        for d in range(1, nj):
            dev = {"yz": lax.rem(j + d, nj)}
            copy = remote(cbuf.at[it], G.at[it, j], sg.at[it, d], rg.at[it, d], dev)
            copy.start()
            sends.append(copy)
            came = G.at[it, lax.rem(j + nj - d, nj)]
            gather.append(remote(cbuf.at[it], came, sg.at[it, d], rg.at[it, d], dev))
        for n, (t, s) in enumerate(((0, 0), (3, 7))):
            for c in range(4):
                for h in range(4):
                    r0 = h * 8 * PLANE + c * 32 + t * 8 + s
                    f = None if it == 0 else X[pl.ds(r0, 8, stride=PLANE), :]
                    for k in range(SWEEPS):
                        term = y[k] * U[k + 1, pl.ds(PLANE + r0, 8, stride=PLANE), :]
                        f = term if f is None else f + term
                    FS[it, 2 + n, pl.ds(c * 32 + h * 8, 8), :] = f
        faces = []
        for src, dst, dev in ((1, 0, right), (0, 1, left), (3, 2, upper), (2, 3, lower)):
            copy = remote(FS.at[it, src], FR.at[it, dst], sf.at[it, dst], rf.at[it, dst], dev)
            copy.start()
            faces.append(copy)
        sends.extend(faces)

        def gather_x(x, carry):
            f = None if it == 0 else tiles(X[rows(x), :])
            for k in range(SWEEPS):
                term = splat(y[k]) * tiles(U[k + 1, rows(x + 1), :])
                f = term if f is None else f + term
            if it == 0:
                X[rows(x), :] = f.reshape(PLANE, 128)
                u = tiles(W[rows(x + 1), :]) - splat(a) * tiles(U[8, rows(x + 1), :])
                u = u - splat(b) * tiles(U[7, rows(x + 1), :])
                U[1, rows(x + 1), :] = (splat(-y[7]) * u).reshape(PLANE, 128)
            else:
                for c in range(4):
                    for t in range(4):
                        fst[c, pl.ds(x * 32 + t, 8, stride=4), :] = f[c, t]
            return carry

        lax.fori_loop(0, 32, gather_x, 0, unroll=4)
        if it == ITERS - 1:
            out_copy = pltpu.make_async_copy(fst, xpre, out_sem)
            out_copy.start()

        for copy in gather:
            copy.wait_recv()
        for sx in range(ni):
            lo, hi = zero, zero
            for ty in range(nj):
                wt = wsp[sx, ty]
                lo = lo + wt * G[it, ty, 0:8, :]
                hi = hi + wt * G[it, ty, 8:16, :]
            PB[it, sx, 0:8, :] = lo
            PB[it, sx, 8:16, :] = hi
        R[it, i] = PB[it, i]
        parts = []
        for d in range(1, ni):
            to = lax.rem(i + d, ni)
            copy = remote(PB.at[it, to], R.at[it, i], sr.at[it, d], rr.at[it, d], {"gx": to})
            copy.start()
            sends.append(copy)
            came = R.at[it, lax.rem(i + ni - d, ni)]
            parts.append(remote(PB.at[it, to], came, sr.at[it, d], rr.at[it, d], {"gx": to}))
        for copy in parts:
            copy.wait_recv()
        own = R[it, 0]
        for n in range(1, ni):
            own = own + R[it, n]
        CS[it] = own
        nbr = []
        for dst, dev in ((0, right), (1, left), (2, upper), (3, lower)):
            copy = remote(CS.at[it], CR.at[it, dst], sc.at[it, dst], rc.at[it, dst], dev)
            copy.start()
            nbr.append(copy)
        sends.extend(nbr)

        def row(block, c, chunk):
            return block[c * 4 + chunk : c * 4 + chunk + 1, :]

        def along_y(block, c0, c1):
            out = []
            for chunk in range(4):
                p = row(block, c0, chunk)[None, None]
                q = row(block, c1, chunk)[None, None]
                out.append((1.0 - wy) * p + wy * q)
            return jnp.concatenate(out, axis=0)

        def along_x(block, c0, c1):
            out = []
            for chunk in range(4):
                out.append((1.0 - wx8) * row(block, c0, chunk) + wx8 * row(block, c1, chunk))
            return jnp.concatenate(out, axis=0)

        for copy in faces:
            copy.wait_recv()
        for copy in nbr:
            copy.wait_recv()
        sq = zero
        for n, (fun, c0, c1, d0, d1, sign, has) in enumerate((
            (along_y, 0, 1, 2, 3, -1.0, has_left),
            (along_y, 2, 3, 0, 1, 1.0, has_right),
            (along_x, 0, 2, 1, 3, -1.0, has_lower),
            (along_x, 1, 3, 0, 2, 1.0, has_upper),
        )):
            mine = FS[it, n] + fun(own, c0, c1).reshape(PLANE, 128)
            theirs = FR[it, n] + fun(CR[it, n], d0, d1).reshape(PLANE, 128)
            jump = (mine - theirs) * (sign * has)
            JMP[n] = jump
            if sign > 0:
                sq = sq + jnp.sum((jump * jump).reshape(16, 8, 128), axis=0)
        TS[it, 0] = sq
        T1[it, i] = sq
        some = []
        for d in range(1, ni):
            dev = {"gx": lax.rem(i + d, ni)}
            copy = remote(TS.at[it, 0], T1.at[it, i], s1.at[it, d], r1.at[it, d], dev)
            copy.start()
            sends.append(copy)
            came = T1.at[it, lax.rem(i + ni - d, ni)]
            some.append(remote(TS.at[it, 0], came, s1.at[it, d], r1.at[it, d], dev))

        def share():
            for copy in some:
                copy.wait_recv()
            part = T1[it, 0]
            for n in range(1, ni):
                part = part + T1[it, n]
            TS[it, 1] = part
            T2[it, j] = part
            for d in range(1, nj):
                dev = {"yz": lax.rem(j + d, nj)}
                copy = remote(TS.at[it, 1], T2.at[it, j], s2.at[it, d], r2.at[it, d], dev)
                copy.start()
                sends.append(copy)
                came = T2.at[it, lax.rem(j + nj - d, nj)]
                rest.append(remote(TS.at[it, 1], came, s2.at[it, d], r2.at[it, d], dev))

        rest = []
        share()
        if it == 0:
            start = along_y(own, 0, 1)
            slope = along_y(own, 2, 3) - start
            m_start = beside_yz(start)
            m_slope = beside_yz(slope)

            def corrected(x, carry):
                wx = x.astype(F32) / 31.0
                e = start + wx * slope
                beside = m_start + wx * m_slope + 2.0 * e
                diag = tiles(U[0, rows(x + 1), :])
                U[1, rows(x + 1), :] = (
                    tiles(U[1, rows(x + 1), :]) - (diag * e - beside)
                ).reshape(PLANE, 128)
                X[rows(x), :] = (tiles(X[rows(x), :]) + e).reshape(PLANE, 128)
                return carry

            lax.fori_loop(0, 32, corrected, 0)
            U[1, rows(1), :] = U[1, rows(1), :] - (start - slope / 31.0).reshape(PLANE, 128)
            U[1, rows(32), :] = U[1, rows(32), :] - (start + slope * (32.0 / 31.0)).reshape(PLANE, 128)
        for copy in rest:
            copy.wait_recv()
        total = T2[it, 0]
        for n in range(1, nj):
            total = total + T2[it, n]
        count = (ni - 1) * nj * 32 * 512 + ni * 32 * (nj - 1) * 512
        step = 0.5 / jnp.sqrt(total_of(total) / float(count) + 1e-6)
        for n in range(4):
            lam = (JMP[n].reshape(16, 8, 128) * step[None]).reshape(PLANE, 128)
            if it > 0:
                lam = LAM[n] + lam
            LAM[n] = lam
        if it == 0:
            U[1, rows(32), :] = U[1, rows(32), :] - LAM[1]
            U[1, rows(1), :] = U[1, rows(1), :] + LAM[0]
            for n, (t, s, sign) in ((3, (3, 7, -1.0)), (2, (0, 0, 1.0))):
                for c in range(4):
                    for h in range(4):
                        at = pl.ds(PLANE + h * 8 * PLANE + c * 32 + t * 8 + s, 8, stride=PLANE)
                        U[1, at, :] = U[1, at, :] + sign * LAM[n, pl.ds(c * 32 + h * 8, 8), :]
        else:
            corr_out[...] = own
            lamy_out[...] = LAM[3]
            for c in range(4):
                for t in range(4):
                    lamx_out[pl.ds(c * 32 + t, 8, stride=4), :] = LAM[1, pl.ds(c * 32 + t * 8, 8), :]
    for copy in sends:
        copy.wait_send()
    out_copy.wait()


def finish_kernel(xpre, corr, lamx, lamy, vel, mx, my):
    step = pl.program_id(0)
    wide = vel.shape[0]
    wx = (lax.broadcasted_iota(jnp.int32, (wide, 32, 128), 0) + step * wide).astype(F32) / 31.0
    wy = lax.broadcasted_iota(jnp.int32, (wide, 32, 128), 1).astype(F32) / 31.0
    for c in range(4):
        at = pl.ds(c * 128, 128)
        c0, c1, c2, c3 = (corr[n * 4 + c : n * 4 + c + 1, :][None] for n in range(4))
        e = (1.0 - wx) * ((1.0 - wy) * c0 + wy * c1) + wx * ((1.0 - wy) * c2 + wy * c3)
        vel[:, :, at] = xpre[c].reshape(wide, 32, 128) + e

    @pl.when(step == 0)
    def _():
        for c in range(4):
            at = pl.ds(c * 128, 128)
            mx[:, at] = lamx[pl.ds(c * 32, 32), :]
            my[:, at] = lamy[pl.ds(c * 32, 32), :]


def on_device(ni, nj, perm_class, class_drag, force, coarse_inverse, coarse_owner):
    hbm = pl.BlockSpec(memory_space=pl.ANY)
    vmem = pl.BlockSpec(memory_space=pltpu.VMEM)
    smem = pl.BlockSpec(memory_space=pltpu.SMEM)
    dma = pltpu.SemaphoreType.DMA
    xpre, corr, lamx, lamy = pl.pallas_call(
        functools.partial(kernel, ni, nj),
        out_shape=(
            jax.ShapeDtypeStruct((4, 1024, 128), F32),
            jax.ShapeDtypeStruct((16, 128), F32),
            jax.ShapeDtypeStruct((128, 128), F32),
            jax.ShapeDtypeStruct((128, 128), F32),
        ),
        in_specs=[hbm, smem, hbm, hbm, smem],
        out_specs=(hbm, vmem, vmem, vmem),
        scratch_shapes=[
            pltpu.VMEM((SWEEPS + 2, 34 * PLANE, 128), F32),
            pltpu.VMEM((34 * PLANE, 128), F32),
            pltpu.VMEM((32 * PLANE, 128), F32),
            pltpu.VMEM((4, 1024, 128), F32),
            pltpu.VMEM((4, 1024, 128), jnp.int32),
            pltpu.VMEM((16, 8, 128), F32),
            pltpu.VMEM((ni, nj, 8, 128), F32),
            pltpu.SMEM((ni * nj, ni * nj), F32),
            pltpu.VMEM((ITERS, 16, 128), F32),
            pltpu.VMEM((ITERS, nj, 16, 128), F32),
            pltpu.VMEM((ITERS, ni, 16, 128), F32),
            pltpu.VMEM((ITERS, ni, 16, 128), F32),
            pltpu.VMEM((ITERS, 4, PLANE, 128), F32),
            pltpu.VMEM((ITERS, 4, PLANE, 128), F32),
            pltpu.VMEM((ITERS, 16, 128), F32),
            pltpu.VMEM((ITERS, 4, 16, 128), F32),
            pltpu.VMEM((ITERS, 2, 8, 128), F32),
            pltpu.VMEM((ITERS, ni, 8, 128), F32),
            pltpu.VMEM((ITERS, nj, 8, 128), F32),
            pltpu.VMEM((4, PLANE, 128), F32),
            pltpu.VMEM((4, PLANE, 128), F32),
            dma((8,)), dma, dma,
            dma((ITERS, nj)), dma((ITERS, nj)),
            dma((ITERS, ni)), dma((ITERS, ni)),
            dma((ITERS, 4)), dma((ITERS, 4)),
            dma((ITERS, 4)), dma((ITERS, 4)),
            dma((ITERS, ni)), dma((ITERS, ni)),
            dma((ITERS, nj)), dma((ITERS, nj)),
        ],
        compiler_params=pltpu.CompilerParams(
            collective_id=0, has_side_effects=True, vmem_limit_bytes=56 * 2**20
        ),
        name="solve",
    )(perm_class.reshape(1024, 512), class_drag, force.reshape(1024, 512), coarse_inverse, coarse_owner)
    steps, wide = 4, 8
    velocity, mult_x, mult_y = pl.pallas_call(
        finish_kernel,
        grid=(steps,),
        out_shape=(
            jax.ShapeDtypeStruct((32, 32, 512), F32),
            jax.ShapeDtypeStruct((32, 512), F32),
            jax.ShapeDtypeStruct((32, 512), F32),
        ),
        in_specs=[
            pl.BlockSpec((4, 32 * wide, 128), lambda n: (0, n, 0)),
            pl.BlockSpec((16, 128), lambda n: (0, 0)),
            pl.BlockSpec((128, 128), lambda n: (0, 0)),
            pl.BlockSpec((128, 128), lambda n: (0, 0)),
        ],
        out_specs=(
            pl.BlockSpec((wide, 32, 512), lambda n: (n, 0, 0)),
            pl.BlockSpec((32, 512), lambda n: (0, 0)),
            pl.BlockSpec((32, 512), lambda n: (0, 0)),
        ),
        compiler_params=pltpu.CompilerParams(vmem_limit_bytes=16 * 2**20),
        name="finish",
    )(xpre, corr, lamx, lamy)
    return velocity, mult_x[None], mult_y[:, None]


def solution(mesh):
    return jax.shard_map(
        functools.partial(on_device, mesh.shape["gx"], mesh.shape["yz"]),
        mesh=mesh,
        in_specs=(P("gx", "yz", None), P(), P("gx", "yz", None), P(), P()),
        out_specs=(P("gx", "yz", None), P("gx", "yz", None), P("gx", "yz", None)),
        check_vma=False,
    )
```

time: 736 us -> 88.8 us (0.12); the launches traced: 726 us -> 88.5 us
  other arithmetic: 360 us -> 0 us
  waiting for transfers between devices: 143 us -> 0 us
  blocking collectives: 132 us -> 0 us
  Pallas kernels: 0 us -> 83.2 us
  between operations: 59.9 us -> 0.65 us
  starting transfers between devices: 12.6 us -> 0 us
  local copies, waits for them, and re-layouts: 14.2 us -> 4.66 us
    reduce_sum x33 -> x0, other arithmetic: 253 us -> none  [the longest x16 187 us: inner_solve(): alpha = norm_now / jnp.sum(direction * image)]
    psum x2 -> x0, blocking collectives: 132 us -> none  [on_device(): total = lax.psum(local_total, ('gx', 'yz'))]
    all_gather x2 -> x0, waiting for transfers between devices: 125 us -> none  [on_device(): lax.all_gather(corners, ('gx', 'yz'), axis=0, tiled=True)]
    pallas_call x0 -> x2, Pallas kernels: none -> 83.2 us  [the longest x1 81.1 us: on_device(): pl.pallas_call(functools.partial(kernel, ni, nj), out_shape=(jax.ShapeDty...]
    add x20 -> x0, other arithmetic: 70.1 us -> none  [the longest x14 47.1 us: inner_solve(): direction = residual + norm_next / norm_now * direction]
    sub x2 -> x0, other arithmetic: 29.5 us -> none  [inner_solve(): residual = right_side - operate(solution, drag_field)]
    ppermute x7 -> x0, waiting for transfers between devices: 18.6 us -> none  [the longest x4 16 us: extended(): after = lax.ppermute(initial, axis, down)]
    ppermute x7 -> x0, starting transfers between devices: 12.6 us -> none  [the longest x4 6.91 us: extended(): after = lax.ppermute(initial, axis, down)]
  transfers between devices with their start and end apart: 9 -> 0, of which waited for: 8 -> 0; matrix products, arithmetic and copies ran while one was open for 1% -> 0% of each run, Pallas kernels for 0% -> 0%
where the time goes in v1:
time: 88.8 us; the launch traced here: 88.5 us
  Pallas kernels  83.2 us (94%)
  local copies, waits for them, and re-layouts  4.66 us (5%)
    pallas_call x1, Pallas kernels, on_device(): pl.pallas_call(functools.partial(kernel, ni, nj), out_shape=(jax.ShapeDty...  81.1 us
    unnamed x9, local copies, waits for them, and re-layouts  4.66 us
    pallas_call x1, Pallas kernels, on_device(): pl.pallas_call(finish_kernel, grid=(steps,), out_shape=(jax.ShapeDtypeStr...  2.11 us

profile of v1, /device:TPU:1, one launch (start us, length us, event | category | flops | bytes accessed | tf_op | source)
XLA Modules:
  0.0 88.5 jit_solution(1497543848164015327)
XLA Ops:
  0.6 81.1 %solve.1 = (f32[4,1024,128]{2,1,0:T(8,128)}, f32[16,128]{1,0:T(8,128)}, f32[128,128]{1,0:T(8,128)}, f32[128,128]{1,0:T(8,128)}) custom-call(s32[1024,512]{1,0:T(8,128)} %bitcast.5, f32[8]{0:T(128)} %drag.1, f32[1024,512]{1,0:T(8,128)} %bitcast.6, f32[128,128]{1,0:T(8,128)} %cinv.1, s32[128]{0:T(128)} %owner.1), custom_call_target="tpu_custom_call" | custom-call | tf_op jit(solution)/shard_map/solve/pallas_call | solution.py:414
  81.7 0.0 copy-start
  81.7 1.6 %copy-done = f32[4,1024,128]{2,1,0:T(8,128)S(1)} copy-done((f32[4,1024,128]{2,1,0:T(8,128)S(1)}, f32[4,1024,128]{2,1,0:T(8,128)}, u32[]{:S(2)}) %copy-start) | copy-done | bytes 2097176
  83.3 0.0 copy-start.1
  83.3 0.8 copy-done.1
  84.2 0.0 copy-start.2
  84.2 0.8 copy-done.2
  85.0 0.0 copy-start.3
  85.0 0.7 copy-done.3
  85.7 2.1 %finish.1 = (f32[32,32,512]{2,1,0:T(8,128)}, f32[32,512]{1,0:T(8,128)}, f32[32,512]{1,0:T(8,128)S(1)}) custom-call(f32[4,1024,128]{2,1,0:T(8,128)S(1)} %copy-done, f32[16,128]{1,0:T(8,128)S(1)} %copy-done.3, f32[128,128]{1,0:T(8,128)S(1)} %copy-done.1, f32[128,128]{1,0:T(8,128)S(1)} %copy-done.2), custom_call_target="tpu_custom_call" | custom-call | tf_op jit(solution)/shard_map/finish/pallas_call | solution.py:460
  87.8 0.7 copy.8
Async XLA Ops:
  81.7 1.6 %copy-start = (f32[4,1024,128]{2,1,0:T(8,128)S(1)}, f32[4,1024,128]{2,1,0:T(8,128)}, u32[]{:S(2)}) copy-start(f32[4,1024,128]{2,1,0:T(8,128)} %get-tuple-element.10.xpre) | copy-start | bytes 6291460
  83.3 0.8 copy-start.1
  84.2 0.8 copy-start.2
  85.0 0.7 copy-start.3

commit v2 on v1

--- a/solution.py
+++ b/solution.py
@@ -13,7 +13,7 @@
 F32 = jnp.float32
 MESH = pl.DeviceIdType.MESH
 PLANE = 128
-UNROLL = 8
+UNROLL = 16
 
 
 def rows(x):
@@ -84,8 +84,8 @@
 def kernel(
     ni, nj, perm, drag, force, cinv, owner,
     xpre, corr_out, lamx_out, lamy_out,
-    U, W, X, fst, pst, cf, wsp, cinv_s, cbuf, G, PB, R, FS, FR, CS, CR, TS, T1, T2, LAM, JMP,
-    in_sem, ci_sem, out_sem, sg, rg, sr, rr, sf, rf, sc, rc, s1, r1, s2, r2,
+    U, W, X, fst, pst, cf, wsp, cinv_s, cbuf, G, PB, R, FS, FR, TS, TR, LAM, JMP,
+    in_sem, ci_sem, sg, rg, sr, rr, sf, rf, st, rt,
 ):
     i = lax.axis_index("gx")
     j = lax.axis_index("yz")
@@ -93,10 +93,13 @@
     plane0 = jnp.zeros((PLANE, 128), F32)
 
     barrier = pltpu.get_barrier_semaphore()
-    for d in range(1, ni):
-        pl.semaphore_signal(barrier, inc=1, device_id={"gx": lax.rem(i + d, ni)}, device_id_type=MESH)
-    for d in range(1, nj):
-        pl.semaphore_signal(barrier, inc=1, device_id={"yz": lax.rem(j + d, nj)}, device_id_type=MESH)
+
+    def greet(n, carry):
+        dev = {"gx": lax.rem(i + n // nj, ni), "yz": lax.rem(j + n % nj, nj)}
+        pl.semaphore_signal(barrier, inc=1, device_id=dev, device_id_type=MESH)
+        return carry
+
+    lax.fori_loop(1, ni * nj, greet, 0)
 
     loads = []
     for c in range(4):
@@ -134,16 +137,6 @@
 
         lax.fori_loop(0, 32, stage, 0, unroll=4)
 
-    weights_copy.wait()
-    for sx in range(ni):
-        row = owner[sx * nj + j]
-
-        def fill(ty, carry, sx=sx, row=row):
-            wsp[sx, ty] = jnp.full((8, 128), cinv_s[row, owner[i * nj + ty]], F32)
-            return carry
-
-        lax.fori_loop(0, nj, fill, 0, unroll=4)
-
     has_right = (i < ni - 1).astype(F32)
     has_left = (i > 0).astype(F32)
     has_upper = (j < nj - 1).astype(F32)
@@ -185,17 +178,17 @@
             y[k] = (z[k] - bv[k + 1] * y[k + 1]) * inv[k]
 
         for n, x in ((0, 0), (1, 31)):
-            f = None if it == 0 else tiles(X[rows(x), :])
-            for k in range(SWEEPS):
-                term = splat(y[k]) * tiles(U[k + 1, rows(x + 1), :])
-                f = term if f is None else f + term
-            FS[it, n] = f.reshape(PLANE, 128)
-            for m, (t, s) in enumerate(((0, 0), (3, 7))):
+            for m, (t, r) in enumerate(((0, 0), (3, 7))):
                 for c in range(4):
-                    cbuf[it, pl.ds((2 * n + m) * 4 + c, 1), :] = f[c, t, s : s + 1, :]
+                    at = c * 32 + t * 8
+                    f = None if it == 0 else X[pl.ds(x * PLANE + at, 8), :]
+                    for k in range(SWEEPS):
+                        term = y[k] * U[k + 1, pl.ds((x + 1) * PLANE + at, 8), :]
+                        f = term if f is None else f + term
+                    cbuf[it, pl.ds((2 * n + m) * 4 + c, 1), :] = f[r : r + 1, :]
         G[it, j] = cbuf[it]
         if it == 0:
-            pl.semaphore_wait(barrier, ni + nj - 2)
+            pl.semaphore_wait(barrier, ni * nj - 1)
         gather = []
         for d in range(1, nj):
             dev = {"yz": lax.rem(j + d, nj)}
@@ -204,53 +197,67 @@
             sends.append(copy)
             came = G.at[it, lax.rem(j + nj - d, nj)]
             gather.append(remote(cbuf.at[it], came, sg.at[it, d], rg.at[it, d], dev))
-        for n, (t, s) in enumerate(((0, 0), (3, 7))):
+        def gather_x(x, carry):
+            f = None if it == 0 else tiles(X[rows(x), :])
+            for k in range(SWEEPS):
+                term = splat(y[k]) * tiles(U[k + 1, rows(x + 1), :])
+                f = term if f is None else f + term
             for c in range(4):
-                for h in range(4):
-                    r0 = h * 8 * PLANE + c * 32 + t * 8 + s
-                    f = None if it == 0 else X[pl.ds(r0, 8, stride=PLANE), :]
-                    for k in range(SWEEPS):
-                        term = y[k] * U[k + 1, pl.ds(PLANE + r0, 8, stride=PLANE), :]
-                        f = term if f is None else f + term
-                    FS[it, 2 + n, pl.ds(c * 32 + h * 8, 8), :] = f
+                FS[it, 2, pl.ds(c * 32 + x, 1), :] = f[c, 0, 0:1, :]
+                FS[it, 3, pl.ds(c * 32 + x, 1), :] = f[c, 3, 7:8, :]
+            if it == 0:
+                X[rows(x), :] = f.reshape(PLANE, 128)
+                u = tiles(W[rows(x + 1), :]) - splat(a) * tiles(U[8, rows(x + 1), :])
+                u = u - splat(b) * tiles(U[7, rows(x + 1), :])
+                U[1, rows(x + 1), :] = (splat(-y[7]) * u).reshape(PLANE, 128)
+            else:
+                X[rows(x), :] = f.reshape(PLANE, 128)
+                for c in range(4):
+                    for t in range(4):
+                        xpre[c, pl.ds(x * 32 + t, 8, stride=4), :] = f[c, t]
+            return carry
+
+        lax.fori_loop(0, 32, gather_x, 0, unroll=4)
+        FS[it, 0] = X[rows(0), :]
+        FS[it, 1] = X[rows(31), :]
         faces = []
         for src, dst, dev in ((1, 0, right), (0, 1, left), (3, 2, upper), (2, 3, lower)):
             copy = remote(FS.at[it, src], FR.at[it, dst], sf.at[it, dst], rf.at[it, dst], dev)
             copy.start()
             faces.append(copy)
         sends.extend(faces)
-
-        def gather_x(x, carry):
-            f = None if it == 0 else tiles(X[rows(x), :])
-            for k in range(SWEEPS):
-                term = splat(y[k]) * tiles(U[k + 1, rows(x + 1), :])
-                f = term if f is None else f + term
-            if it == 0:
-                X[rows(x), :] = f.reshape(PLANE, 128)
-                u = tiles(W[rows(x + 1), :]) - splat(a) * tiles(U[8, rows(x + 1), :])
-                u = u - splat(b) * tiles(U[7, rows(x + 1), :])
-                U[1, rows(x + 1), :] = (splat(-y[7]) * u).reshape(PLANE, 128)
-            else:
-                for c in range(4):
-                    for t in range(4):
-                        fst[c, pl.ds(x * 32 + t, 8, stride=4), :] = f[c, t]
-            return carry
-
-        lax.fori_loop(0, 32, gather_x, 0, unroll=4)
-        if it == ITERS - 1:
-            out_copy = pltpu.make_async_copy(fst, xpre, out_sem)
-            out_copy.start()
+        if it == 0:
+            weights_copy.wait()
+            for n in range(3):
+                jn = lax.rem(j + nj - 1 + n, nj)
+                for sx in range(ni):
+
+                    def fill(ty, carry, n=n, sx=sx, at=owner[sx * nj + jn]):
+                        wsp[n, sx, ty] = jnp.full((8, 128), cinv_s[at, owner[i * nj + ty]], F32)
+                        return carry
+
+                    lax.fori_loop(0, nj, fill, 0, unroll=4)
 
         for copy in gather:
             copy.wait_recv()
+        sub = lax.broadcasted_iota(jnp.int32, (8, 128), 0) < 4
         for sx in range(ni):
-            lo, hi = zero, zero
-            for ty in range(nj):
-                wt = wsp[sx, ty]
-                lo = lo + wt * G[it, ty, 0:8, :]
-                hi = hi + wt * G[it, ty, 8:16, :]
+
+            def term(ty, acc, sx=sx):
+                lo, hi, down, up = acc
+                g01, g23 = G[it, ty, 0:8, :], G[it, ty, 8:16, :]
+                g13 = jnp.where(sub, pltpu.roll(g01, 4, 0), g23)
+                g02 = jnp.where(sub, g01, pltpu.roll(g23, 4, 0))
+                w = wsp[1, sx, ty]
+                return lo + w * g01, hi + w * g23, down + wsp[0, sx, ty] * g13, up + wsp[2, sx, ty] * g02
+
+            lo, hi, down, up = lax.fori_loop(0, nj, term, (zero,) * 4, unroll=8)
             PB[it, sx, 0:8, :] = lo
             PB[it, sx, 8:16, :] = hi
+            PB[it, (sx + 1) % ni, 16:24, :] = hi
+            PB[it, (sx - 1) % ni, 24:32, :] = lo
+            PB[it, sx, 32:40, :] = down
+            PB[it, sx, 40:48, :] = up
         R[it, i] = PB[it, i]
         parts = []
         for d in range(1, ni):
@@ -260,18 +267,15 @@
             sends.append(copy)
             came = R.at[it, lax.rem(i + ni - d, ni)]
             parts.append(remote(PB.at[it, to], came, sr.at[it, d], rr.at[it, d], {"gx": to}))
+        for copy in faces:
+            copy.wait_recv()
         for copy in parts:
             copy.wait_recv()
-        own = R[it, 0]
+        sums = R[it, 0]
         for n in range(1, ni):
-            own = own + R[it, n]
-        CS[it] = own
-        nbr = []
-        for dst, dev in ((0, right), (1, left), (2, upper), (3, lower)):
-            copy = remote(CS.at[it], CR.at[it, dst], sc.at[it, dst], rc.at[it, dst], dev)
-            copy.start()
-            nbr.append(copy)
-        sends.extend(nbr)
+            sums = sums + R[it, n]
+        own = sums[0:16]
+        other = [sums[16 + 8 * n : 24 + 8 * n] for n in range(4)]
 
         def row(block, c, chunk):
             return block[c * 4 + chunk : c * 4 + chunk + 1, :]
@@ -290,52 +294,33 @@
                 out.append((1.0 - wx8) * row(block, c0, chunk) + wx8 * row(block, c1, chunk))
             return jnp.concatenate(out, axis=0)
 
-        for copy in faces:
-            copy.wait_recv()
-        for copy in nbr:
-            copy.wait_recv()
         sq = zero
-        for n, (fun, c0, c1, d0, d1, sign, has) in enumerate((
-            (along_y, 0, 1, 2, 3, -1.0, has_left),
-            (along_y, 2, 3, 0, 1, 1.0, has_right),
-            (along_x, 0, 2, 1, 3, -1.0, has_lower),
-            (along_x, 1, 3, 0, 2, 1.0, has_upper),
+        for n, (fun, c0, c1, sign, has) in enumerate((
+            (along_y, 0, 1, -1.0, has_left),
+            (along_y, 2, 3, 1.0, has_right),
+            (along_x, 0, 2, -1.0, has_lower),
+            (along_x, 1, 3, 1.0, has_upper),
         )):
             mine = FS[it, n] + fun(own, c0, c1).reshape(PLANE, 128)
-            theirs = FR[it, n] + fun(CR[it, n], d0, d1).reshape(PLANE, 128)
+            theirs = FR[it, n] + fun(other[n], 0, 1).reshape(PLANE, 128)
             jump = (mine - theirs) * (sign * has)
             JMP[n] = jump
             if sign > 0:
                 sq = sq + jnp.sum((jump * jump).reshape(16, 8, 128), axis=0)
-        TS[it, 0] = sq
-        T1[it, i] = sq
-        some = []
-        for d in range(1, ni):
-            dev = {"gx": lax.rem(i + d, ni)}
-            copy = remote(TS.at[it, 0], T1.at[it, i], s1.at[it, d], r1.at[it, d], dev)
-            copy.start()
-            sends.append(copy)
-            came = T1.at[it, lax.rem(i + ni - d, ni)]
-            some.append(remote(TS.at[it, 0], came, s1.at[it, d], r1.at[it, d], dev))
-
-        def share():
-            for copy in some:
-                copy.wait_recv()
-            part = T1[it, 0]
-            for n in range(1, ni):
-                part = part + T1[it, n]
-            TS[it, 1] = part
-            T2[it, j] = part
-            for d in range(1, nj):
-                dev = {"yz": lax.rem(j + d, nj)}
-                copy = remote(TS.at[it, 1], T2.at[it, j], s2.at[it, d], r2.at[it, d], dev)
-                copy.start()
-                sends.append(copy)
-                came = T2.at[it, lax.rem(j + nj - d, nj)]
-                rest.append(remote(TS.at[it, 1], came, s2.at[it, d], r2.at[it, d], dev))
-
-        rest = []
-        share()
+        me = i * nj + j
+        row_sum = jnp.sum(sq, axis=0, keepdims=True)
+        TS[it] = row_sum
+        TR[it, pl.ds(me, 1), :] = row_sum
+
+        def tell(n, carry):
+            dev = {"gx": lax.rem(i + n // nj, ni), "yz": lax.rem(j + n % nj, nj)}
+            remote(TS.at[it], TR.at[it, pl.ds(me, 1)], st.at[it], rt.at[it], dev).start()
+            return carry
+
+        lax.fori_loop(1, ni * nj, tell, 0)
+        all_but_one = TR.at[it, pl.ds(0, ni * nj - 1)]
+        told = remote(all_but_one, all_but_one, st.at[it], rt.at[it], right)
+        sends.append(told)
         if it == 0:
             start = along_y(own, 0, 1)
             slope = along_y(own, 2, 3) - start
@@ -356,11 +341,8 @@
             lax.fori_loop(0, 32, corrected, 0)
             U[1, rows(1), :] = U[1, rows(1), :] - (start - slope / 31.0).reshape(PLANE, 128)
             U[1, rows(32), :] = U[1, rows(32), :] - (start + slope * (32.0 / 31.0)).reshape(PLANE, 128)
-        for copy in rest:
-            copy.wait_recv()
-        total = T2[it, 0]
-        for n in range(1, nj):
-            total = total + T2[it, n]
+        told.wait_recv()
+        total = jnp.sum(TR[it].reshape(ni * nj // 8, 8, 128), axis=0)
         count = (ni - 1) * nj * 32 * 512 + ni * 32 * (nj - 1) * 512
         step = 0.5 / jnp.sqrt(total_of(total) / float(count) + 1e-6)
         for n in range(4):
@@ -384,26 +366,25 @@
                     lamx_out[pl.ds(c * 32 + t, 8, stride=4), :] = LAM[1, pl.ds(c * 32 + t * 8, 8), :]
     for copy in sends:
         copy.wait_send()
-    out_copy.wait()
-
-
-def finish_kernel(xpre, corr, lamx, lamy, vel, mx, my):
+
+
+def finish_kernel(wide, xpre, corr, lamx, lamy, vel, mx, my):
     step = pl.program_id(0)
-    wide = vel.shape[0]
     wx = (lax.broadcasted_iota(jnp.int32, (wide, 32, 128), 0) + step * wide).astype(F32) / 31.0
     wy = lax.broadcasted_iota(jnp.int32, (wide, 32, 128), 1).astype(F32) / 31.0
     for c in range(4):
         at = pl.ds(c * 128, 128)
         c0, c1, c2, c3 = (corr[n * 4 + c : n * 4 + c + 1, :][None] for n in range(4))
         e = (1.0 - wx) * ((1.0 - wy) * c0 + wy * c1) + wx * ((1.0 - wy) * c2 + wy * c3)
-        vel[:, :, at] = xpre[c].reshape(wide, 32, 128) + e
+        part = xpre[c, pl.ds(pl.multiple_of(step * 32 * wide, 32 * wide), 32 * wide), :]
+        vel[:, :, at] = part.reshape(wide, 32, 128) + e
 
     @pl.when(step == 0)
     def _():
         for c in range(4):
             at = pl.ds(c * 128, 128)
             mx[:, at] = lamx[pl.ds(c * 32, 32), :]
-            my[:, at] = lamy[pl.ds(c * 32, 32), :]
+            my[:, :, at] = lamy[pl.ds(c * 32, 32), :].reshape(32, 1, 128)
 
 
 def on_device(ni, nj, perm_class, class_drag, force, coarse_inverse, coarse_owner):
@@ -414,13 +395,13 @@
     xpre, corr, lamx, lamy = pl.pallas_call(
         functools.partial(kernel, ni, nj),
         out_shape=(
-            jax.ShapeDtypeStruct((4, 1024, 128), F32),
-            jax.ShapeDtypeStruct((16, 128), F32),
-            jax.ShapeDtypeStruct((128, 128), F32),
-            jax.ShapeDtypeStruct((128, 128), F32),
+            pltpu.VMEM((4, 1024, 128), F32),
+            pltpu.VMEM((16, 128), F32),
+            pltpu.VMEM((128, 128), F32),
+            pltpu.VMEM((128, 128), F32),
         ),
         in_specs=[hbm, smem, hbm, hbm, smem],
-        out_specs=(hbm, vmem, vmem, vmem),
+        out_specs=(vmem, vmem, vmem, vmem),
         scratch_shapes=[
             pltpu.VMEM((SWEEPS + 2, 34 * PLANE, 128), F32),
             pltpu.VMEM((34 * PLANE, 128), F32),
@@ -428,28 +409,23 @@
             pltpu.VMEM((4, 1024, 128), F32),
             pltpu.VMEM((4, 1024, 128), jnp.int32),
             pltpu.VMEM((16, 8, 128), F32),
-            pltpu.VMEM((ni, nj, 8, 128), F32),
+            pltpu.VMEM((3, ni, nj, 8, 128), F32),
             pltpu.SMEM((ni * nj, ni * nj), F32),
             pltpu.VMEM((ITERS, 16, 128), F32),
             pltpu.VMEM((ITERS, nj, 16, 128), F32),
-            pltpu.VMEM((ITERS, ni, 16, 128), F32),
-            pltpu.VMEM((ITERS, ni, 16, 128), F32),
+            pltpu.VMEM((ITERS, ni, 48, 128), F32),
+            pltpu.VMEM((ITERS, ni, 48, 128), F32),
             pltpu.VMEM((ITERS, 4, PLANE, 128), F32),
             pltpu.VMEM((ITERS, 4, PLANE, 128), F32),
-            pltpu.VMEM((ITERS, 16, 128), F32),
-            pltpu.VMEM((ITERS, 4, 16, 128), F32),
-            pltpu.VMEM((ITERS, 2, 8, 128), F32),
-            pltpu.VMEM((ITERS, ni, 8, 128), F32),
-            pltpu.VMEM((ITERS, nj, 8, 128), F32),
+            pltpu.VMEM((ITERS, 1, 128), F32),
+            pltpu.VMEM((ITERS, ni * nj, 128), F32),
             pltpu.VMEM((4, PLANE, 128), F32),
             pltpu.VMEM((4, PLANE, 128), F32),
-            dma((8,)), dma, dma,
+            dma((8,)), dma,
             dma((ITERS, nj)), dma((ITERS, nj)),
             dma((ITERS, ni)), dma((ITERS, ni)),
             dma((ITERS, 4)), dma((ITERS, 4)),
-            dma((ITERS, 4)), dma((ITERS, 4)),
-            dma((ITERS, ni)), dma((ITERS, ni)),
-            dma((ITERS, nj)), dma((ITERS, nj)),
+            dma((ITERS,)), dma((ITERS,)),
         ],
         compiler_params=pltpu.CompilerParams(
             collective_id=0, has_side_effects=True, vmem_limit_bytes=56 * 2**20
@@ -458,28 +434,23 @@
     )(perm_class.reshape(1024, 512), class_drag, force.reshape(1024, 512), coarse_inverse, coarse_owner)
     steps, wide = 4, 8
     velocity, mult_x, mult_y = pl.pallas_call(
-        finish_kernel,
+        functools.partial(finish_kernel, wide),
         grid=(steps,),
         out_shape=(
             jax.ShapeDtypeStruct((32, 32, 512), F32),
             jax.ShapeDtypeStruct((32, 512), F32),
-            jax.ShapeDtypeStruct((32, 512), F32),
+            jax.ShapeDtypeStruct((32, 1, 512), F32),
         ),
-        in_specs=[
-            pl.BlockSpec((4, 32 * wide, 128), lambda n: (0, n, 0)),
-            pl.BlockSpec((16, 128), lambda n: (0, 0)),
-            pl.BlockSpec((128, 128), lambda n: (0, 0)),
-            pl.BlockSpec((128, 128), lambda n: (0, 0)),
-        ],
+        in_specs=[vmem] * 4,
         out_specs=(
             pl.BlockSpec((wide, 32, 512), lambda n: (n, 0, 0)),
             pl.BlockSpec((32, 512), lambda n: (0, 0)),
-            pl.BlockSpec((32, 512), lambda n: (0, 0)),
+            pl.BlockSpec((32, 1, 512), lambda n: (0, 0, 0)),
         ),
         compiler_params=pltpu.CompilerParams(vmem_limit_bytes=16 * 2**20),
         name="finish",
     )(xpre, corr, lamx, lamy)
-    return velocity, mult_x[None], mult_y[:, None]
+    return velocity, mult_x[None], mult_y
 
 
 def solution(mesh):

time: 88.8 us -> 75.3 us (0.85)
  Pallas kernels: 83.2 us -> 74.6 us
  local copies, waits for them, and re-layouts: 4.66 us -> 0 us
    pallas_call x2, Pallas kernels: 83.2 us -> 74.6 us  [the longest x1 72.5 us: on_device(): pl.pallas_call(functools.partial(kernel, ni, nj), out_shape=(pltpu.VMEM((...]
    unnamed x9 -> x0, local copies, waits for them, and re-layouts: 4.66 us -> none
where the time goes in v2:
time: 75.3 us; the launch traced here: 75.2 us
  Pallas kernels  74.6 us (99%)
    pallas_call x1, Pallas kernels, on_device(): pl.pallas_call(functools.partial(kernel, ni, nj), out_shape=(pltpu.VMEM((...  72.5 us
    pallas_call x1, Pallas kernels, on_device(): pl.pallas_call(functools.partial(finish_kernel, wide), grid=(steps,), out...  2.07 us

profile of v2, /device:TPU:1, one launch (start us, length us, event | category | flops | bytes accessed | tf_op | source)
XLA Modules:
  0.0 75.2 jit_solution(4917084604278992721)
XLA Ops:
  0.6 72.5 %solve.1 = (f32[4,1024,128]{2,1,0:T(8,128)S(1)}, f32[16,128]{1,0:T(8,128)S(1)}, f32[128,128]{1,0:T(8,128)S(1)}, f32[128,128]{1,0:T(8,128)S(1)}) custom-call(s32[1024,512]{1,0:T(8,128)} %bitcast.3, f32[8]{0:T(128)} %drag.1, f32[1024,512]{1,0:T(8,128)} %bitcast.4, f32[128,128]{1,0:T(8,128)} %cinv.1, s32[128]{0:T(128)} %owner.1), custom_call_target="tpu_custom_call" | custom-call | tf_op jit(solution)/shard_map/solve/pallas_call | solution.py:395
  73.1 2.1 %finish.1 = (f32[32,32,512]{2,1,0:T(8,128)}, f32[32,512]{1,0:T(8,128)}, f32[32,1,512]{2,1,0:T(1,128)}) custom-call(f32[4,1024,128]{2,1,0:T(8,128)S(1)} %get-tuple-element.10.xpre, f32[16,128]{1,0:T(8,128)S(1)} %get-tuple-element.11.corr, f32[128,128]{1,0:T(8,128)S(1)} %get-tuple-element.12.lamx, f32[128,128]{1,0:T(8,128)S(1)} %get-tuple-element.13.lamy), custom_call_target="tpu_custom_call" | custom-call | tf_op jit(solution)/shard_map/finish/pallas_call | solution.py:436

commit v3 on v2

--- a/solution.py
+++ b/solution.py
@@ -12,6 +12,7 @@
 ITERS = 2
 F32 = jnp.float32
 MESH = pl.DeviceIdType.MESH
+BF16 = jnp.bfloat16
 PLANE = 128
 UNROLL = 16
 
@@ -25,18 +26,33 @@
 
 
 def beside_yz(cur):
-    lane = lax.broadcasted_iota(jnp.int32, (4, 4, 8, 128), 3)
-    sub = lax.broadcasted_iota(jnp.int32, (4, 1, 8, 128), 2)
-    gap = jnp.zeros((1, 4, 8, 128), F32)
-    up = pltpu.roll(cur, 1, 3)
-    down = pltpu.roll(cur, 127, 3)
-    left = jnp.where(lane == 0, jnp.concatenate([gap, up[:-1]], axis=0), up)
-    right = jnp.where(lane == 127, jnp.concatenate([down[1:], gap], axis=0), down)
-    before = jnp.where(sub == 0, 0.0, pltpu.roll(cur[:, 3:4], 1, 2))
-    after = jnp.where(sub == 7, 0.0, pltpu.roll(cur[:, 0:1], 7, 2))
-    low = jnp.concatenate([before, cur[:, 0:3]], axis=1)
-    high = jnp.concatenate([cur[:, 1:4], after], axis=1)
-    return (high + low) + (left + right)
+    lane = lax.broadcasted_iota(jnp.int32, (4, 1, 8, 128), 3)
+    sub = lax.broadcasted_iota(jnp.int32, (1, 4, 8, 128), 2)
+    left = jnp.where(lane == 0, 0.0, pltpu.roll(cur[:, 3:4], 1, 3))
+    right = jnp.where(lane == 127, 0.0, pltpu.roll(cur[:, 0:1], 127, 3))
+    before = jnp.where(sub == 0, 0.0, pltpu.roll(cur[3:4], 1, 2))
+    after = jnp.where(sub == 7, 0.0, pltpu.roll(cur[0:1], 7, 2))
+    low = jnp.concatenate([before, cur[0:3]], axis=0)
+    high = jnp.concatenate([cur[1:4], after], axis=0)
+    nearer = jnp.concatenate([left, cur[:, 0:3]], axis=1)
+    further = jnp.concatenate([cur[:, 1:4], right], axis=1)
+    return (high + low) + (nearer + further)
+
+
+def three(a):
+    high = a.astype(BF16)
+    rest = a - high.astype(F32)
+    middle = rest.astype(BF16)
+    return high, middle, (rest - middle.astype(F32)).astype(BF16)
+
+
+def reorder(a, perm, back):
+    dims = (((1,), (1 if back else 0,)), ((), ()))
+    out = None
+    for piece in three(a):
+        term = lax.dot_general(piece, perm, dims, preferred_element_type=F32)
+        out = term if out is None else out + term
+    return out
 
 
 def total_of(a):
@@ -48,43 +64,68 @@
     return a[None, None]
 
 
+def part(x, t):
+    return pl.ds(pl.multiple_of(x * PLANE, PLANE) + t * 32, 32)
+
+
+def quad(value):
+    return value.reshape(4, 8, 128)
+
+
 def sweep_pass(k, first, a, b, U, W):
-    def fresh(x):
-        u = tiles(W[rows(x), :]) - splat(a) * tiles(U[k, rows(x), :])
-        u = u - splat(b) * tiles(U[k - 1, rows(x), :])
-        U[k + 1, rows(x), :] = u.reshape(PLANE, 128)
+    lane = lax.broadcasted_iota(jnp.int32, (1, 8, 128), 2)
+    sub = lax.broadcasted_iota(jnp.int32, (4, 8, 128), 1)
+
+    def fresh(x, t):
+        u = quad(W[part(x, t), :]) - a[None] * quad(U[k, part(x, t), :])
+        u = u - b[None] * quad(U[k - 1, part(x, t), :])
+        U[k + 1, part(x, t), :] = u.reshape(32, 128)
         return u
 
     def step(x, acc):
         uu, uw = acc
-        if first:
-            above = tiles(U[k + 1, rows(x + 2), :])
-        else:
-            above = fresh(x + 2)
-        cur = tiles(U[k + 1, rows(x + 1), :])
-        below = tiles(U[k + 1, rows(x), :])
-        w = tiles(U[0, rows(x + 1), :]) * cur - ((above + below) + beside_yz(cur))
-        W[rows(x + 1), :] = w.reshape(PLANE, 128)
-        return uu + jnp.sum(cur * cur, axis=(0, 1)), uw + jnp.sum(cur * w, axis=(0, 1))
+        for t in range(4):
+            if first:
+                above = quad(U[k + 1, part(x + 2, t), :])
+            else:
+                above = fresh(x + 2, t)
+            cur = quad(U[k + 1, part(x + 1, t), :])
+            below = quad(U[k + 1, part(x, t), :])
+            low = quad(U[k + 1, part(x + 1, (t + 3) % 4), :])
+            high = quad(U[k + 1, part(x + 1, (t + 1) % 4), :])
+            if t == 0:
+                low = jnp.where(sub == 0, 0.0, pltpu.roll(low, 1, 1))
+            if t == 3:
+                high = jnp.where(sub == 7, 0.0, pltpu.roll(high, 7, 1))
+            left = jnp.where(lane == 0, 0.0, pltpu.roll(cur[3:4], 1, 2))
+            right = jnp.where(lane == 127, 0.0, pltpu.roll(cur[0:1], 127, 2))
+            left = jnp.concatenate([left, cur[0:3]], axis=0)
+            right = jnp.concatenate([cur[1:4], right], axis=0)
+            beside = ((above + below) + (high + low)) + (left + right)
+            w = quad(U[0, part(x + 1, t), :]) * cur - beside
+            W[part(x + 1, t), :] = w.reshape(32, 128)
+            uu, uw = uu + cur * cur, uw + cur * w
+        return uu, uw
 
     if not first:
-        fresh(1)
-    zero = jnp.zeros((8, 128), F32)
+        for t in range(4):
+            fresh(1, t)
+    zero = jnp.zeros((4, 8, 128), F32)
     uu, uw = lax.fori_loop(0, 32, step, (zero, zero), unroll=UNROLL)
-    g = total_of(uu)
-    return g, total_of(uw) / g
+    g = total_of(jnp.sum(uu, axis=0))
+    return g, total_of(jnp.sum(uw, axis=0)) / g
 
 
 def y_weights(width):
-    t = lax.broadcasted_iota(jnp.int32, (1, 4, 8, 128), 1)
-    s = lax.broadcasted_iota(jnp.int32, (1, 4, 8, 128), 2)
+    t = lax.broadcasted_iota(jnp.int32, (4, 1, 8, 128), 0)
+    s = lax.broadcasted_iota(jnp.int32, (4, 1, 8, 128), 2)
     return (4 * s + t).astype(F32) / (width - 1)
 
 
 def kernel(
     ni, nj, perm, drag, force, cinv, owner,
     xpre, corr_out, lamx_out, lamy_out,
-    U, W, X, fst, pst, cf, wsp, cinv_s, cbuf, G, PB, R, FS, FR, TS, TR, LAM, JMP,
+    U, W, X, fst, pst, cf, wsp, cinv_s, cbuf, G, PB, R, FS, FR, TS, TR, LAM, JMP, PM, CC,
     in_sem, ci_sem, sg, rg, sr, rr, sf, rf, st, rt,
 ):
     i = lax.axis_index("gx")
@@ -101,14 +142,19 @@
 
     lax.fori_loop(1, ni * nj, greet, 0)
 
-    loads = []
-    for c in range(4):
-        cols = pl.ds(c * 128, 128)
-        loads.append((
-            pltpu.make_async_copy(perm.at[:, cols], pst.at[c], in_sem.at[2 * c]),
-            pltpu.make_async_copy(force.at[:, cols], fst.at[c], in_sem.at[2 * c + 1]),
-        ))
-        for copy in loads[-1]:
+    wide = 8
+
+    def chunk_copies(n):
+        at = pl.ds(pl.multiple_of(n * wide * 32, wide * 32), wide * 32)
+        out = []
+        for c in range(4):
+            cols = pl.ds(c * 128, 128)
+            out.append(pltpu.make_async_copy(perm.at[at, cols], pst.at[c, at], in_sem.at[n, c]))
+            out.append(pltpu.make_async_copy(force.at[at, cols], fst.at[c, at], in_sem.at[n, 4 + c]))
+        return out
+
+    for n in range(32 // wide):
+        for copy in chunk_copies(n):
             copy.start()
     weights_copy = pltpu.make_async_copy(cinv, cinv_s, ci_sem)
     weights_copy.start()
@@ -118,24 +164,43 @@
         U[k, rows(33), :] = plane0
     W[rows(33), :] = plane0
 
+    for n in range(4):
+        zin = lax.broadcasted_iota(jnp.int32, (512, 128), 0)
+        lane = lax.broadcasted_iota(jnp.int32, (512, 128), 1)
+        PM[:, pl.ds(n * 128, 128)] = jnp.where(zin == 4 * lane + n, 1.0, 0.0).astype(BF16)
+
     level = [6.0 + drag[c] for c in range(CLASSES)]
-    for c in range(4):
-        for copy in loads[c]:
+
+    def stage(n, carry):
+        for copy in chunk_copies(n):
             copy.wait()
-
-        def stage(x, carry, c=c):
-            base = pl.multiple_of(x * 32, 32)
+        perm_matrix = PM[...]
+
+        def gathered(ref):
+            out = []
+            for x in range(wide):
+                for t in range(4):
+                    at = pl.ds(n * wide * 32 + x * 32 + t, 8, stride=4)
+                    out.append(jnp.concatenate([ref[c, at, :] for c in range(4)], axis=1))
+            return jnp.concatenate(out, axis=0)
+
+        classes = gathered(pst).astype(F32).astype(BF16)
+        classes = jnp.dot(classes, perm_matrix, preferred_element_type=F32)
+        field = reorder(gathered(fst), perm_matrix, False)
+        for x in range(wide):
             for t in range(4):
-                cls = pst[c, pl.ds(base + t, 8, stride=4), :]
-                b0, b1, b2 = (cls & 1) != 0, (cls & 2) != 0, (cls & 4) != 0
-                pairs = [jnp.where(b0, level[n + 1], level[n]) for n in range(0, 8, 2)]
-                quads = [jnp.where(b1, pairs[1], pairs[0]), jnp.where(b1, pairs[3], pairs[2])]
-                at = pl.ds(pl.multiple_of((x + 1) * PLANE + c * 32 + t * 8, 8), 8)
-                U[0, at, :] = jnp.where(b2, quads[1], quads[0])
-                U[1, at, :] = fst[c, pl.ds(base + t, 8, stride=4), :]
-            return carry
-
-        lax.fori_loop(0, 32, stage, 0, unroll=4)
+                for k in range(4):
+                    r, l = slice(x * 32 + t * 8, x * 32 + t * 8 + 8), slice(k * 128, k * 128 + 128)
+                    at = pl.ds(pl.multiple_of((n * wide + x + 1) * PLANE, PLANE) + t * 32 + k * 8, 8)
+                    cls = classes[r, l].astype(jnp.int32)
+                    b0, b1, b2 = (cls & 1) != 0, (cls & 2) != 0, (cls & 4) != 0
+                    pairs = [jnp.where(b0, level[m + 1], level[m]) for m in range(0, 8, 2)]
+                    quads = [jnp.where(b1, pairs[1], pairs[0]), jnp.where(b1, pairs[3], pairs[2])]
+                    U[0, at, :] = jnp.where(b2, quads[1], quads[0])
+                    U[1, at, :] = field[r, l]
+        return carry
+
+    lax.fori_loop(0, 32 // wide, stage, 0)
 
     has_right = (i < ni - 1).astype(F32)
     has_left = (i > 0).astype(F32)
@@ -180,7 +245,7 @@
         for n, x in ((0, 0), (1, 31)):
             for m, (t, r) in enumerate(((0, 0), (3, 7))):
                 for c in range(4):
-                    at = c * 32 + t * 8
+                    at = t * 32 + c * 8
                     f = None if it == 0 else X[pl.ds(x * PLANE + at, 8), :]
                     for k in range(SWEEPS):
                         term = y[k] * U[k + 1, pl.ds((x + 1) * PLANE + at, 8), :]
@@ -203,8 +268,8 @@
                 term = splat(y[k]) * tiles(U[k + 1, rows(x + 1), :])
                 f = term if f is None else f + term
             for c in range(4):
-                FS[it, 2, pl.ds(c * 32 + x, 1), :] = f[c, 0, 0:1, :]
-                FS[it, 3, pl.ds(c * 32 + x, 1), :] = f[c, 3, 7:8, :]
+                FS[it, 2, pl.ds(c * 32 + x, 1), :] = f[0, c, 0:1, :]
+                FS[it, 3, pl.ds(c * 32 + x, 1), :] = f[3, c, 7:8, :]
             if it == 0:
                 X[rows(x), :] = f.reshape(PLANE, 128)
                 u = tiles(W[rows(x + 1), :]) - splat(a) * tiles(U[8, rows(x + 1), :])
@@ -212,9 +277,6 @@
                 U[1, rows(x + 1), :] = (splat(-y[7]) * u).reshape(PLANE, 128)
             else:
                 X[rows(x), :] = f.reshape(PLANE, 128)
-                for c in range(4):
-                    for t in range(4):
-                        xpre[c, pl.ds(x * 32 + t, 8, stride=4), :] = f[c, t]
             return carry
 
         lax.fori_loop(0, 32, gather_x, 0, unroll=4)
@@ -237,6 +299,25 @@
                         return carry
 
                     lax.fori_loop(0, nj, fill, 0, unroll=4)
+
+        else:
+
+            def restore(n, carry):
+                field = []
+                for x in range(wide):
+                    for t in range(4):
+                        at = pl.multiple_of((n * wide + x) * PLANE, PLANE) + t * 32
+                        field.append(jnp.concatenate([X[pl.ds(at + k * 8, 8), :] for k in range(4)], axis=1))
+                field = reorder(jnp.concatenate(field, axis=0), PM[...], True)
+                for x in range(wide):
+                    for t in range(4):
+                        for c in range(4):
+                            at = pl.ds((n * wide + x) * 32 + t, 8, stride=4)
+                            r = x * 32 + t * 8
+                            xpre[c, at, :] = field[r : r + 8, c * 128 : c * 128 + 128]
+                return carry
+
+            lax.fori_loop(0, 32 // wide, restore, 0)
 
         for copy in gather:
             copy.wait_recv()
@@ -286,7 +367,7 @@
                 p = row(block, c0, chunk)[None, None]
                 q = row(block, c1, chunk)[None, None]
                 out.append((1.0 - wy) * p + wy * q)
-            return jnp.concatenate(out, axis=0)
+            return jnp.concatenate(out, axis=1)
 
         def along_x(block, c0, c1):
             out = []
@@ -341,6 +422,12 @@
             lax.fori_loop(0, 32, corrected, 0)
             U[1, rows(1), :] = U[1, rows(1), :] - (start - slope / 31.0).reshape(PLANE, 128)
             U[1, rows(32), :] = U[1, rows(32), :] - (start + slope * (32.0 / 31.0)).reshape(PLANE, 128)
+        if it == ITERS - 1:
+            CC[...] = jnp.zeros((8, 512), F32)
+            for c in range(4):
+                for k in range(4):
+                    CC[pl.ds(c, 1), pl.ds(k * 128, 128)] = row(own, c, k)
+            corr_out[...] = reorder(CC[...], PM[...], True)
         told.wait_recv()
         total = jnp.sum(TR[it].reshape(ni * nj // 8, 8, 128), axis=0)
         count = (ni - 1) * nj * 32 * 512 + ni * 32 * (nj - 1) * 512
@@ -356,14 +443,18 @@
             for n, (t, s, sign) in ((3, (3, 7, -1.0)), (2, (0, 0, 1.0))):
                 for c in range(4):
                     for h in range(4):
-                        at = pl.ds(PLANE + h * 8 * PLANE + c * 32 + t * 8 + s, 8, stride=PLANE)
+                        at = pl.ds(PLANE + h * 8 * PLANE + t * 32 + c * 8 + s, 8, stride=PLANE)
                         U[1, at, :] = U[1, at, :] + sign * LAM[n, pl.ds(c * 32 + h * 8, 8), :]
         else:
-            corr_out[...] = own
-            lamy_out[...] = LAM[3]
+            lam_x = LAM[1].reshape(4, 4, 8, 128)
+            lam_x = jnp.concatenate([lam_x[:, k].reshape(32, 128) for k in range(4)], axis=1)
+            lam_y = jnp.concatenate([LAM[3, pl.ds(k * 32, 32), :] for k in range(4)], axis=1)
+            both = reorder(jnp.concatenate([lam_x, lam_y], axis=0), PM[...], True)
             for c in range(4):
+                lamy_out[pl.ds(c * 32, 32), :] = both[32:64, c * 128 : c * 128 + 128]
                 for t in range(4):
-                    lamx_out[pl.ds(c * 32 + t, 8, stride=4), :] = LAM[1, pl.ds(c * 32 + t * 8, 8), :]
+                    part_of = both[t * 8 : t * 8 + 8, c * 128 : c * 128 + 128]
+                    lamx_out[pl.ds(c * 32 + t, 8, stride=4), :] = part_of
     for copy in sends:
         copy.wait_send()
 
@@ -374,7 +465,7 @@
     wy = lax.broadcasted_iota(jnp.int32, (wide, 32, 128), 1).astype(F32) / 31.0
     for c in range(4):
         at = pl.ds(c * 128, 128)
-        c0, c1, c2, c3 = (corr[n * 4 + c : n * 4 + c + 1, :][None] for n in range(4))
+        c0, c1, c2, c3 = (corr[n : n + 1, at][None] for n in range(4))
         e = (1.0 - wx) * ((1.0 - wy) * c0 + wy * c1) + wx * ((1.0 - wy) * c2 + wy * c3)
         part = xpre[c, pl.ds(pl.multiple_of(step * 32 * wide, 32 * wide), 32 * wide), :]
         vel[:, :, at] = part.reshape(wide, 32, 128) + e
@@ -396,7 +487,7 @@
         functools.partial(kernel, ni, nj),
         out_shape=(
             pltpu.VMEM((4, 1024, 128), F32),
-            pltpu.VMEM((16, 128), F32),
+            pltpu.VMEM((8, 512), F32),
             pltpu.VMEM((128, 128), F32),
             pltpu.VMEM((128, 128), F32),
         ),
@@ -421,7 +512,9 @@
             pltpu.VMEM((ITERS, ni * nj, 128), F32),
             pltpu.VMEM((4, PLANE, 128), F32),
             pltpu.VMEM((4, PLANE, 128), F32),
-            dma((8,)), dma,
+            pltpu.VMEM((512, 512), BF16),
+            pltpu.VMEM((8, 512), F32),
+            dma((4, 8)), dma,
             dma((ITERS, nj)), dma((ITERS, nj)),
             dma((ITERS, ni)), dma((ITERS, ni)),
             dma((ITERS, 4)), dma((ITERS, 4)),

time: 75.3 us -> 74.9 us (level)
  no operation moved by 1% of the time
where the time goes in v3:
time: 74.9 us; the launch traced here: 74.8 us
  Pallas kernels  74.1 us (99%)
    pallas_call x1, Pallas kernels, on_device(): pl.pallas_call(functools.partial(kernel, ni, nj), out_shape=(pltpu.VMEM((...  72.1 us
    pallas_call x1, Pallas kernels, on_device(): pl.pallas_call(functools.partial(finish_kernel, wide), grid=(steps,), out...  2.06 us

profile of v3, /device:TPU:1, one launch (start us, length us, event | category | flops | bytes accessed | tf_op | source)
XLA Modules:
  0.0 74.8 jit_solution(1119156806463873827)
XLA Ops:
  0.6 72.1 %solve.1 = (f32[4,1024,128]{2,1,0:T(8,128)S(1)}, f32[8,512]{1,0:T(8,128)S(1)}, f32[128,128]{1,0:T(8,128)S(1)}, f32[128,128]{1,0:T(8,128)S(1)}) custom-call(s32[1024,512]{1,0:T(8,128)} %bitcast.3, f32[8]{0:T(128)} %drag.1, f32[1024,512]{1,0:T(8,128)} %bitcast.4, f32[128,128]{1,0:T(8,128)} %cinv.1, s32[128]{0:T(128)} %owner.1), custom_call_target="tpu_custom_call" | custom-call | tf_op jit(solution)/shard_map/solve/pallas_call | solution.py:486
  72.7 2.1 %finish.1 = (f32[32,32,512]{2,1,0:T(8,128)}, f32[32,512]{1,0:T(8,128)}, f32[32,1,512]{2,1,0:T(1,128)}) custom-call(f32[4,1024,128]{2,1,0:T(8,128)S(1)} %get-tuple-element.10.xpre, f32[8,512]{1,0:T(8,128)S(1)} %get-tuple-element.11.corr, f32[128,128]{1,0:T(8,128)S(1)} %get-tuple-element.12.lamx, f32[128,128]{1,0:T(8,128)S(1)} %get-tuple-element.13.lamy), custom_call_target="tpu_custom_call" | custom-call | tf_op jit(solution)/shard_map/finish/pallas_call | solution.py:529

commit v4 on v3

--- a/solution.py
+++ b/solution.py
@@ -14,7 +14,7 @@
 MESH = pl.DeviceIdType.MESH
 BF16 = jnp.bfloat16
 PLANE = 128
-UNROLL = 16
+UNROLL = 32
 
 
 def rows(x):
@@ -124,7 +124,7 @@
 
 def kernel(
     ni, nj, perm, drag, force, cinv, owner,
-    xpre, corr_out, lamx_out, lamy_out,
+    xpre, lamx_out, lamy_out,
     U, W, X, fst, pst, cf, wsp, cinv_s, cbuf, G, PB, R, FS, FR, TS, TR, LAM, JMP, PM, CC,
     in_sem, ci_sem, sg, rg, sr, rr, sf, rf, st, rt,
 ):
@@ -169,7 +169,10 @@
         lane = lax.broadcasted_iota(jnp.int32, (512, 128), 1)
         PM[:, pl.ds(n * 128, 128)] = jnp.where(zin == 4 * lane + n, 1.0, 0.0).astype(BF16)
 
-    level = [6.0 + drag[c] for c in range(CLASSES)]
+    lane8 = lax.broadcasted_iota(jnp.int32, (8, 128), 1)
+    level = zero
+    for c in range(CLASSES):
+        level = jnp.where(lane8 == c, 6.0 + drag[c], level)
 
     def stage(n, carry):
         for copy in chunk_copies(n):
@@ -193,10 +196,7 @@
                     r, l = slice(x * 32 + t * 8, x * 32 + t * 8 + 8), slice(k * 128, k * 128 + 128)
                     at = pl.ds(pl.multiple_of((n * wide + x + 1) * PLANE, PLANE) + t * 32 + k * 8, 8)
                     cls = classes[r, l].astype(jnp.int32)
-                    b0, b1, b2 = (cls & 1) != 0, (cls & 2) != 0, (cls & 4) != 0
-                    pairs = [jnp.where(b0, level[m + 1], level[m]) for m in range(0, 8, 2)]
-                    quads = [jnp.where(b1, pairs[1], pairs[0]), jnp.where(b1, pairs[3], pairs[2])]
-                    U[0, at, :] = jnp.where(b2, quads[1], quads[0])
+                    U[0, at, :] = jnp.take_along_axis(level, cls, axis=1, mode="promise_in_bounds")
                     U[1, at, :] = field[r, l]
         return carry
 
@@ -210,6 +210,15 @@
     wx8 = lax.broadcasted_iota(jnp.int32, (32, 128), 0).astype(F32) / 31.0
     right, left = {"gx": lax.rem(i + 1, ni)}, {"gx": lax.rem(i + ni - 1, ni)}
     upper, lower = {"yz": lax.rem(j + 1, nj)}, {"yz": lax.rem(j + nj - 1, nj)}
+    ring = (2, 1, 3, 0)
+    gx_of = [lax.rem(i // 2 + ax, ni // 2) * 2 + lax.rem(i % 2 + core, 2) for ax in ring[-ni // 2 :] for core in (1, 0)]
+    yz_of = [lax.rem(j // 4 + az, nj // 4) * 4 + lax.rem(j % 4 + ay, 4) for az in ring[-nj // 4 :] for ay in ring]
+    far = []
+    for p in range(ni):
+        for q in range(nj):
+            hops = sum((2, 1, 1, 0)[n] for n in (p // 2, q // 4, q % 4))
+            far.append((-hops, p, q))
+    everyone = [{"gx": gx_of[p], "yz": yz_of[q]} for _, p, q in sorted(far)[:-1] if (p, q) != (ni - 1, nj - 1)]
     sends = []
 
     def remote(src, dst, ssem, rsem, dev):
@@ -255,7 +264,7 @@
         if it == 0:
             pl.semaphore_wait(barrier, ni * nj - 1)
         gather = []
-        for d in range(1, nj):
+        for d in sorted(range(1, nj), key=lambda d: -abs((d + 2) % 4 - 2) - abs((d // 4 + 2) % 4 - 2)):
             dev = {"yz": lax.rem(j + d, nj)}
             copy = remote(cbuf.at[it], G.at[it, j], sg.at[it, d], rg.at[it, d], dev)
             copy.start()
@@ -393,12 +402,8 @@
         TS[it] = row_sum
         TR[it, pl.ds(me, 1), :] = row_sum
 
-        def tell(n, carry):
-            dev = {"gx": lax.rem(i + n // nj, ni), "yz": lax.rem(j + n % nj, nj)}
-            remote(TS.at[it], TR.at[it, pl.ds(me, 1)], st.at[it], rt.at[it], dev).start()
-            return carry
-
-        lax.fori_loop(1, ni * nj, tell, 0)
+        for other_one in everyone:
+            remote(TS.at[it], TR.at[it, pl.ds(me, 1)], st.at[it], rt.at[it], other_one).start()
         all_but_one = TR.at[it, pl.ds(0, ni * nj - 1)]
         told = remote(all_but_one, all_but_one, st.at[it], rt.at[it], right)
         sends.append(told)
@@ -427,7 +432,20 @@
             for c in range(4):
                 for k in range(4):
                     CC[pl.ds(c, 1), pl.ds(k * 128, 128)] = row(own, c, k)
-            corr_out[...] = reorder(CC[...], PM[...], True)
+            corr = reorder(CC[...], PM[...], True)
+            wy2 = lax.broadcasted_iota(jnp.int32, (32, 128), 0).astype(F32) / 31.0
+            for c in range(4):
+                c0, c1, c2, c3 = (corr[n : n + 1, c * 128 : c * 128 + 128] for n in range(4))
+                begin = (1.0 - wy2) * c0 + wy2 * c1
+                end = (1.0 - wy2) * c2 + wy2 * c3
+
+                def add(x, carry, c=c, begin=begin, end=end):
+                    wx = x.astype(F32) / 31.0
+                    at = pl.ds(pl.multiple_of(x * 32, 32), 32)
+                    xpre[c, at, :] = xpre[c, at, :] + ((1.0 - wx) * begin + wx * end)
+                    return carry
+
+                lax.fori_loop(0, 32, add, 0, unroll=8)
         told.wait_recv()
         total = jnp.sum(TR[it].reshape(ni * nj // 8, 8, 128), axis=0)
         count = (ni - 1) * nj * 32 * 512 + ni * 32 * (nj - 1) * 512
@@ -459,23 +477,20 @@
         copy.wait_send()
 
 
-def finish_kernel(wide, xpre, corr, lamx, lamy, vel, mx, my):
-    step = pl.program_id(0)
-    wx = (lax.broadcasted_iota(jnp.int32, (wide, 32, 128), 0) + step * wide).astype(F32) / 31.0
-    wy = lax.broadcasted_iota(jnp.int32, (wide, 32, 128), 1).astype(F32) / 31.0
+def finish_kernel(field, lamx, lamy, vel, mx, my, my_s, sems):
+    copies = []
     for c in range(4):
         at = pl.ds(c * 128, 128)
-        c0, c1, c2, c3 = (corr[n : n + 1, at][None] for n in range(4))
-        e = (1.0 - wx) * ((1.0 - wy) * c0 + wy * c1) + wx * ((1.0 - wy) * c2 + wy * c3)
-        part = xpre[c, pl.ds(pl.multiple_of(step * 32 * wide, 32 * wide), 32 * wide), :]
-        vel[:, :, at] = part.reshape(wide, 32, 128) + e
-
-    @pl.when(step == 0)
-    def _():
-        for c in range(4):
-            at = pl.ds(c * 128, 128)
-            mx[:, at] = lamx[pl.ds(c * 32, 32), :]
-            my[:, :, at] = lamy[pl.ds(c * 32, 32), :].reshape(32, 1, 128)
+        copies.append(pltpu.make_async_copy(field.at[c], vel.at[:, at], sems.at[0, c]))
+        copies.append(pltpu.make_async_copy(lamx.at[pl.ds(c * 32, 32)], mx.at[:, at], sems.at[1, c]))
+    for copy in copies:
+        copy.start()
+    for c in range(4):
+        my_s[:, :, pl.ds(c * 128, 128)] = lamy[pl.ds(c * 32, 32), :].reshape(32, 1, 128)
+    copies.append(pltpu.make_async_copy(my_s, my, sems.at[2, 0]))
+    copies[-1].start()
+    for copy in copies:
+        copy.wait()
 
 
 def on_device(ni, nj, perm_class, class_drag, force, coarse_inverse, coarse_owner):
@@ -483,16 +498,15 @@
     vmem = pl.BlockSpec(memory_space=pltpu.VMEM)
     smem = pl.BlockSpec(memory_space=pltpu.SMEM)
     dma = pltpu.SemaphoreType.DMA
-    xpre, corr, lamx, lamy = pl.pallas_call(
+    xpre, lamx, lamy = pl.pallas_call(
         functools.partial(kernel, ni, nj),
         out_shape=(
             pltpu.VMEM((4, 1024, 128), F32),
-            pltpu.VMEM((8, 512), F32),
             pltpu.VMEM((128, 128), F32),
             pltpu.VMEM((128, 128), F32),
         ),
         in_specs=[hbm, smem, hbm, hbm, smem],
-        out_specs=(vmem, vmem, vmem, vmem),
+        out_specs=(vmem, vmem, vmem),
         scratch_shapes=[
             pltpu.VMEM((SWEEPS + 2, 34 * PLANE, 128), F32),
             pltpu.VMEM((34 * PLANE, 128), F32),
@@ -525,25 +539,20 @@
         ),
         name="solve",
     )(perm_class.reshape(1024, 512), class_drag, force.reshape(1024, 512), coarse_inverse, coarse_owner)
-    steps, wide = 4, 8
     velocity, mult_x, mult_y = pl.pallas_call(
-        functools.partial(finish_kernel, wide),
-        grid=(steps,),
+        finish_kernel,
         out_shape=(
-            jax.ShapeDtypeStruct((32, 32, 512), F32),
+            jax.ShapeDtypeStruct((1024, 512), F32),
             jax.ShapeDtypeStruct((32, 512), F32),
             jax.ShapeDtypeStruct((32, 1, 512), F32),
         ),
-        in_specs=[vmem] * 4,
-        out_specs=(
-            pl.BlockSpec((wide, 32, 512), lambda n: (n, 0, 0)),
-            pl.BlockSpec((32, 512), lambda n: (0, 0)),
-            pl.BlockSpec((32, 1, 512), lambda n: (0, 0, 0)),
-        ),
-        compiler_params=pltpu.CompilerParams(vmem_limit_bytes=16 * 2**20),
+        in_specs=[vmem] * 3,
+        out_specs=(hbm, hbm, hbm),
+        scratch_shapes=[pltpu.VMEM((32, 1, 512), F32), dma((3, 4))],
+        compiler_params=pltpu.CompilerParams(vmem_limit_bytes=4 * 2**20),
         name="finish",
-    )(xpre, corr, lamx, lamy)
-    return velocity, mult_x[None], mult_y
+    )(xpre, lamx, lamy)
+    return velocity.reshape(32, 32, 512), mult_x[None], mult_y
 
 
 def solution(mesh):

time: 74.9 us -> 68.5 us (0.915)
  Pallas kernels: 74.1 us -> 67.7 us
    pallas_call x1, Pallas kernels: 72.1 us -> 66.3 us  [on_device(): pl.pallas_call(functools.partial(kernel, ni, nj), out_shape=(pltpu.VMEM((...]
where the time goes in v4:
time: 68.5 us; the launch traced here: 68.4 us
  Pallas kernels  67.7 us (99%)
    pallas_call x1, Pallas kernels, on_device(): pl.pallas_call(functools.partial(kernel, ni, nj), out_shape=(pltpu.VMEM((...  66.3 us
    pallas_call x1, Pallas kernels, on_device(): pl.pallas_call(finish_kernel, out_shape=(jax.ShapeDtypeStruct((1024, 512)...  1.45 us

profile of v4, /device:TPU:1, one launch (start us, length us, event | category | flops | bytes accessed | tf_op | source)
XLA Modules:
  0.0 68.4 jit_solution(1259220580702683900)
XLA Ops:
  0.6 66.3 %solve.1 = (f32[4,1024,128]{2,1,0:T(8,128)S(1)}, f32[128,128]{1,0:T(8,128)S(1)}, f32[128,128]{1,0:T(8,128)S(1)}) custom-call(s32[1024,512]{1,0:T(8,128)} %bitcast.4, f32[8]{0:T(128)} %drag.1, f32[1024,512]{1,0:T(8,128)} %bitcast.5, f32[128,128]{1,0:T(8,128)} %cinv.1, s32[128]{0:T(128)} %owner.1), custom_call_target="tpu_custom_call" | custom-call | tf_op jit(solution)/shard_map/solve/pallas_call | solution.py:501
  66.9 1.4 %finish.1 = (f32[1024,512]{1,0:T(8,128)}, f32[32,512]{1,0:T(8,128)}, f32[32,1,512]{2,1,0:T(1,128)}) custom-call(f32[4,1024,128]{2,1,0:T(8,128)S(1)} %get-tuple-element.9.field, f32[128,128]{1,0:T(8,128)S(1)} %get-tuple-element.10.lamx, f32[128,128]{1,0:T(8,128)S(1)} %get-tuple-element.11.lamy), custom_call_target="tpu_custom_call" | custom-call | tf_op jit(solution)/shard_map/finish/pallas_call | solution.py:542

commit v5 on v4

--- a/solution.py
+++ b/solution.py
@@ -125,7 +125,7 @@
 def kernel(
     ni, nj, perm, drag, force, cinv, owner,
     xpre, lamx_out, lamy_out,
-    U, W, X, fst, pst, cf, wsp, cinv_s, cbuf, G, PB, R, FS, FR, TS, TR, LAM, JMP, PM, CC,
+    U, W, X, fst, pst, cf, wsp, cinv_s, cbuf, G, PB, R, FS, FR, TS, TR, LAM, JMP, PM, CC, RL,
     in_sem, ci_sem, sg, rg, sr, rr, sf, rf, st, rt,
 ):
     i = lax.axis_index("gx")
@@ -134,13 +134,6 @@
     plane0 = jnp.zeros((PLANE, 128), F32)
 
     barrier = pltpu.get_barrier_semaphore()
-
-    def greet(n, carry):
-        dev = {"gx": lax.rem(i + n // nj, ni), "yz": lax.rem(j + n % nj, nj)}
-        pl.semaphore_signal(barrier, inc=1, device_id=dev, device_id_type=MESH)
-        return carry
-
-    lax.fori_loop(1, ni * nj, greet, 0)
 
     wide = 8
 
@@ -158,6 +151,13 @@
             copy.start()
     weights_copy = pltpu.make_async_copy(cinv, cinv_s, ci_sem)
     weights_copy.start()
+
+    def greet(n, carry):
+        dev = {"gx": lax.rem(i + n // nj, ni), "yz": lax.rem(j + n % nj, nj)}
+        pl.semaphore_signal(barrier, inc=1, device_id=dev, device_id_type=MESH)
+        return carry
+
+    lax.fori_loop(1, ni * nj, greet, 0)
 
     for k in range(SWEEPS + 2):
         U[k, rows(0), :] = plane0
@@ -228,28 +228,25 @@
 
     for it in range(ITERS):
         g, a = sweep_pass(0, True, zero, zero, U, W)
-        cf[0], cf[8] = a, zero
+        one = jnp.ones((8, 128), F32)
 
         def body(k, carry):
-            g, a, b = carry
+            g, a, b, pivot, z = carry
+            inv = 1.0 / (a - b * pivot)
+            cf[k - 1] = inv
+            cf[7 + k] = b
+            cf[15 + k] = z
             gn, an = sweep_pass(k, False, a, b, U, W)
-            bn = gn / g
-            cf[k] = an
-            cf[8 + k] = bn
-            return gn, an, bn
-
-        g, a, b = lax.fori_loop(1, SWEEPS, body, (g, a, zero))
-
-        av = [cf[k] for k in range(SWEEPS)]
-        bv = [cf[8 + k] for k in range(SWEEPS)]
-        inv, z = [1.0 / av[0]], [jnp.ones((8, 128), F32)]
-        for k in range(1, SWEEPS):
-            z.append(-z[k - 1] * inv[k - 1])
-            inv.append(1.0 / (av[k] - bv[k] * inv[k - 1]))
+            return gn, an, gn / g, inv, -z * inv
+
+        g, a, b, pivot, z = lax.fori_loop(1, SWEEPS, body, (g, a, zero, zero, one))
+
         y = [None] * SWEEPS
-        y[SWEEPS - 1] = z[SWEEPS - 1] * inv[SWEEPS - 1]
+        y[SWEEPS - 1] = z / (a - b * pivot)
+        above = b
         for k in range(SWEEPS - 2, -1, -1):
-            y[k] = (z[k] - bv[k + 1] * y[k + 1]) * inv[k]
+            y[k] = (cf[16 + k] - above * y[k + 1]) * cf[k]
+            above = cf[8 + k]
 
         for n, x in ((0, 0), (1, 31)):
             for m, (t, r) in enumerate(((0, 0), (3, 7))):
@@ -406,7 +403,7 @@
             remote(TS.at[it], TR.at[it, pl.ds(me, 1)], st.at[it], rt.at[it], other_one).start()
         all_but_one = TR.at[it, pl.ds(0, ni * nj - 1)]
         told = remote(all_but_one, all_but_one, st.at[it], rt.at[it], right)
-        sends.append(told)
+        arrived, sends = sends, [told]
         if it == 0:
             start = along_y(own, 0, 1)
             slope = along_y(own, 2, 3) - start
@@ -428,6 +425,12 @@
             U[1, rows(1), :] = U[1, rows(1), :] - (start - slope / 31.0).reshape(PLANE, 128)
             U[1, rows(32), :] = U[1, rows(32), :] - (start + slope * (32.0 / 31.0)).reshape(PLANE, 128)
         if it == ITERS - 1:
+            faces_in = []
+            for ref in (LAM, JMP):
+                face = ref[1].reshape(4, 4, 8, 128)
+                faces_in.append(jnp.concatenate([face[:, k].reshape(32, 128) for k in range(4)], axis=1))
+                faces_in.append(jnp.concatenate([ref[3, pl.ds(k * 32, 32), :] for k in range(4)], axis=1))
+            RL[...] = reorder(jnp.concatenate(faces_in, axis=0), PM[...], True)
             CC[...] = jnp.zeros((8, 512), F32)
             for c in range(4):
                 for k in range(4):
@@ -446,16 +449,15 @@
                     return carry
 
                 lax.fori_loop(0, 32, add, 0, unroll=8)
+        for copy in arrived:
+            copy.wait_send()
         told.wait_recv()
         total = jnp.sum(TR[it].reshape(ni * nj // 8, 8, 128), axis=0)
         count = (ni - 1) * nj * 32 * 512 + ni * 32 * (nj - 1) * 512
         step = 0.5 / jnp.sqrt(total_of(total) / float(count) + 1e-6)
-        for n in range(4):
-            lam = (JMP[n].reshape(16, 8, 128) * step[None]).reshape(PLANE, 128)
-            if it > 0:
-                lam = LAM[n] + lam
-            LAM[n] = lam
         if it == 0:
+            for n in range(4):
+                LAM[n] = (JMP[n].reshape(16, 8, 128) * step[None]).reshape(PLANE, 128)
             U[1, rows(32), :] = U[1, rows(32), :] - LAM[1]
             U[1, rows(1), :] = U[1, rows(1), :] + LAM[0]
             for n, (t, s, sign) in ((3, (3, 7, -1.0)), (2, (0, 0, 1.0))):
@@ -464,15 +466,13 @@
                         at = pl.ds(PLANE + h * 8 * PLANE + t * 32 + c * 8 + s, 8, stride=PLANE)
                         U[1, at, :] = U[1, at, :] + sign * LAM[n, pl.ds(c * 32 + h * 8, 8), :]
         else:
-            lam_x = LAM[1].reshape(4, 4, 8, 128)
-            lam_x = jnp.concatenate([lam_x[:, k].reshape(32, 128) for k in range(4)], axis=1)
-            lam_y = jnp.concatenate([LAM[3, pl.ds(k * 32, 32), :] for k in range(4)], axis=1)
-            both = reorder(jnp.concatenate([lam_x, lam_y], axis=0), PM[...], True)
             for c in range(4):
-                lamy_out[pl.ds(c * 32, 32), :] = both[32:64, c * 128 : c * 128 + 128]
-                for t in range(4):
-                    part_of = both[t * 8 : t * 8 + 8, c * 128 : c * 128 + 128]
-                    lamx_out[pl.ds(c * 32 + t, 8, stride=4), :] = part_of
+                cols = pl.ds(c * 128, 128)
+                for h in range(4):
+                    both = RL[pl.ds(h * 8, 8), cols] + step * RL[pl.ds(64 + h * 8, 8), cols]
+                    lamx_out[pl.ds(c * 32 + h, 8, stride=4), :] = both
+                    both = RL[pl.ds(32 + h * 8, 8), cols] + step * RL[pl.ds(96 + h * 8, 8), cols]
+                    lamy_out[pl.ds(c * 32 + h * 8, 8), :] = both
     for copy in sends:
         copy.wait_send()
 
@@ -513,7 +513,7 @@
             pltpu.VMEM((32 * PLANE, 128), F32),
             pltpu.VMEM((4, 1024, 128), F32),
             pltpu.VMEM((4, 1024, 128), jnp.int32),
-            pltpu.VMEM((16, 8, 128), F32),
+            pltpu.VMEM((24, 8, 128), F32),
             pltpu.VMEM((3, ni, nj, 8, 128), F32),
             pltpu.SMEM((ni * nj, ni * nj), F32),
             pltpu.VMEM((ITERS, 16, 128), F32),
@@ -528,6 +528,7 @@
             pltpu.VMEM((4, PLANE, 128), F32),
             pltpu.VMEM((512, 512), BF16),
             pltpu.VMEM((8, 512), F32),
+            pltpu.VMEM((128, 512), F32),
             dma((4, 8)), dma,
             dma((ITERS, nj)), dma((ITERS, nj)),
             dma((ITERS, ni)), dma((ITERS, ni)),

time: 68.5 us -> 66.8 us (0.975)
  Pallas kernels: 67.7 us -> 66 us
    pallas_call x1, Pallas kernels: 66.3 us -> 64.6 us  [on_device(): pl.pallas_call(functools.partial(kernel, ni, nj), out_shape=(pltpu.VMEM((...]
where the time goes in v5:
time: 66.8 us; the launch traced here: 66.7 us
  Pallas kernels  66 us (99%)
    pallas_call x1, Pallas kernels, on_device(): pl.pallas_call(functools.partial(kernel, ni, nj), out_shape=(pltpu.VMEM((...  64.6 us
    pallas_call x1, Pallas kernels, on_device(): pl.pallas_call(finish_kernel, out_shape=(jax.ShapeDtypeStruct((1024, 512)...  1.45 us

profile of v5, /device:TPU:1, one launch (start us, length us, event | category | flops | bytes accessed | tf_op | source)
XLA Modules:
  0.0 66.7 jit_solution(9657383206610657712)
XLA Ops:
  0.6 64.6 %solve.1 = (f32[4,1024,128]{2,1,0:T(8,128)S(1)}, f32[128,128]{1,0:T(8,128)S(1)}, f32[128,128]{1,0:T(8,128)S(1)}) custom-call(s32[1024,512]{1,0:T(8,128)} %bitcast.4, f32[8]{0:T(128)} %drag.1, f32[1024,512]{1,0:T(8,128)} %bitcast.5, f32[128,128]{1,0:T(8,128)} %cinv.1, s32[128]{0:T(128)} %owner.1), custom_call_target="tpu_custom_call" | custom-call | tf_op jit(solution)/shard_map/solve/pallas_call | solution.py:501
  65.2 1.4 %finish.1 = (f32[1024,512]{1,0:T(8,128)}, f32[32,512]{1,0:T(8,128)}, f32[32,1,512]{2,1,0:T(1,128)}) custom-call(f32[4,1024,128]{2,1,0:T(8,128)S(1)} %get-tuple-element.9.field, f32[128,128]{1,0:T(8,128)S(1)} %get-tuple-element.10.lamx, f32[128,128]{1,0:T(8,128)S(1)} %get-tuple-element.11.lamy), custom_call_target="tpu_custom_call" | custom-call | tf_op jit(solution)/shard_map/finish/pallas_call | solution.py:543

commit v6 on v5

--- a/solution.py
+++ b/solution.py
@@ -187,9 +187,11 @@
                     out.append(jnp.concatenate([ref[c, at, :] for c in range(4)], axis=1))
             return jnp.concatenate(out, axis=0)
 
-        classes = gathered(pst).astype(F32).astype(BF16)
-        classes = jnp.dot(classes, perm_matrix, preferred_element_type=F32)
-        field = reorder(gathered(fst), perm_matrix, False)
+        pieces = (gathered(pst).astype(F32).astype(BF16),) + three(gathered(fst))
+        size = wide * 32
+        moved = jnp.dot(jnp.concatenate(pieces, axis=0), perm_matrix, preferred_element_type=F32)
+        classes = moved[0:size]
+        field = moved[size : 2 * size] + moved[2 * size : 3 * size] + moved[3 * size : 4 * size]
         for x in range(wide):
             for t in range(4):
                 for k in range(4):
@@ -347,7 +349,7 @@
             PB[it, sx, 40:48, :] = up
         R[it, i] = PB[it, i]
         parts = []
-        for d in range(1, ni):
+        for d in sorted(range(1, ni), key=lambda d: -abs((d // 2 + 2) % 4 - 2)):
             to = lax.rem(i + d, ni)
             copy = remote(PB.at[it, to], R.at[it, i], sr.at[it, d], rr.at[it, d], {"gx": to})
             copy.start()

time: 66.8 us -> 67 us (level)
  no operation moved by 1% of the time
where the time goes in v6:
time: 67 us; the launch traced here: 66.9 us
  Pallas kernels  66.2 us (99%)
    pallas_call x1, Pallas kernels, on_device(): pl.pallas_call(functools.partial(kernel, ni, nj), out_shape=(pltpu.VMEM((...  64.8 us
    pallas_call x1, Pallas kernels, on_device(): pl.pallas_call(finish_kernel, out_shape=(jax.ShapeDtypeStruct((1024, 512)...  1.45 us

profile of v6, /device:TPU:1, one launch (start us, length us, event | category | flops | bytes accessed | tf_op | source)
XLA Modules:
  0.0 66.9 jit_solution(2553916401763336786)
XLA Ops:
  0.6 64.8 %solve.1 = (f32[4,1024,128]{2,1,0:T(8,128)S(1)}, f32[128,128]{1,0:T(8,128)S(1)}, f32[128,128]{1,0:T(8,128)S(1)}) custom-call(s32[1024,512]{1,0:T(8,128)} %bitcast.4, f32[8]{0:T(128)} %drag.1, f32[1024,512]{1,0:T(8,128)} %bitcast.5, f32[128,128]{1,0:T(8,128)} %cinv.1, s32[128]{0:T(128)} %owner.1), custom_call_target="tpu_custom_call" | custom-call | tf_op jit(solution)/shard_map/solve/pallas_call | solution.py:503
  65.4 1.4 %finish.1 = (f32[1024,512]{1,0:T(8,128)}, f32[32,512]{1,0:T(8,128)}, f32[32,1,512]{2,1,0:T(1,128)}) custom-call(f32[4,1024,128]{2,1,0:T(8,128)S(1)} %get-tuple-element.9.field, f32[128,128]{1,0:T(8,128)S(1)} %get-tuple-element.10.lamx, f32[128,128]{1,0:T(8,128)S(1)} %get-tuple-element.11.lamy), custom_call_target="tpu_custom_call" | custom-call | tf_op jit(solution)/shard_map/finish/pallas_call | solution.py:545

commit v7 on v6

--- a/solution.py
+++ b/solution.py
@@ -152,12 +152,10 @@
     weights_copy = pltpu.make_async_copy(cinv, cinv_s, ci_sem)
     weights_copy.start()
 
-    def greet(n, carry):
-        dev = {"gx": lax.rem(i + n // nj, ni), "yz": lax.rem(j + n % nj, nj)}
-        pl.semaphore_signal(barrier, inc=1, device_id=dev, device_id_type=MESH)
-        return carry
-
-    lax.fori_loop(1, ni * nj, greet, 0)
+    for d in range(1, ni):
+        pl.semaphore_signal(barrier, inc=1, device_id={"gx": lax.rem(i + d, ni)}, device_id_type=MESH)
+    for d in range(1, nj):
+        pl.semaphore_signal(barrier, inc=1, device_id={"yz": lax.rem(j + d, nj)}, device_id_type=MESH)
 
     for k in range(SWEEPS + 2):
         U[k, rows(0), :] = plane0
@@ -261,7 +259,7 @@
                     cbuf[it, pl.ds((2 * n + m) * 4 + c, 1), :] = f[r : r + 1, :]
         G[it, j] = cbuf[it]
         if it == 0:
-            pl.semaphore_wait(barrier, ni * nj - 1)
+            pl.semaphore_wait(barrier, ni + nj - 2)
         gather = []
         for d in sorted(range(1, nj), key=lambda d: -abs((d + 2) % 4 - 2) - abs((d // 4 + 2) % 4 - 2)):
             dev = {"yz": lax.rem(j + d, nj)}

time: 67 us -> 65.2 us (0.973)
  Pallas kernels: 66.2 us -> 64.4 us
    pallas_call x1, Pallas kernels: 64.8 us -> 63 us  [on_device(): pl.pallas_call(functools.partial(kernel, ni, nj), out_shape=(pltpu.VMEM((...]
where the time goes in v7:
time: 65.2 us; the launch traced here: 65 us
  Pallas kernels  64.4 us (99%)
    pallas_call x1, Pallas kernels, on_device(): pl.pallas_call(functools.partial(kernel, ni, nj), out_shape=(pltpu.VMEM((...  63 us
    pallas_call x1, Pallas kernels, on_device(): pl.pallas_call(finish_kernel, out_shape=(jax.ShapeDtypeStruct((1024, 512)...  1.45 us

profile of v7, /device:TPU:1, one launch (start us, length us, event | category | flops | bytes accessed | tf_op | source)
XLA Modules:
  0.0 65.0 jit_solution(17901286055903446894)
XLA Ops:
  0.6 63.0 %solve.1 = (f32[4,1024,128]{2,1,0:T(8,128)S(1)}, f32[128,128]{1,0:T(8,128)S(1)}, f32[128,128]{1,0:T(8,128)S(1)}) custom-call(s32[1024,512]{1,0:T(8,128)} %bitcast.4, f32[8]{0:T(128)} %drag.1, f32[1024,512]{1,0:T(8,128)} %bitcast.5, f32[128,128]{1,0:T(8,128)} %cinv.1, s32[128]{0:T(128)} %owner.1), custom_call_target="tpu_custom_call" | custom-call | tf_op jit(solution)/shard_map/solve/pallas_call | solution.py:501
  63.6 1.4 %finish.1 = (f32[1024,512]{1,0:T(8,128)}, f32[32,512]{1,0:T(8,128)}, f32[32,1,512]{2,1,0:T(1,128)}) custom-call(f32[4,1024,128]{2,1,0:T(8,128)S(1)} %get-tuple-element.9.field, f32[128,128]{1,0:T(8,128)S(1)} %get-tuple-element.10.lamx, f32[128,128]{1,0:T(8,128)S(1)} %get-tuple-element.11.lamy), custom_call_target="tpu_custom_call" | custom-call | tf_op jit(solution)/shard_map/finish/pallas_call | solution.py:543

commit v8 on v7

--- a/solution.py
+++ b/solution.py
@@ -97,10 +97,10 @@
                 low = jnp.where(sub == 0, 0.0, pltpu.roll(low, 1, 1))
             if t == 3:
                 high = jnp.where(sub == 7, 0.0, pltpu.roll(high, 7, 1))
-            left = jnp.where(lane == 0, 0.0, pltpu.roll(cur[3:4], 1, 2))
-            right = jnp.where(lane == 127, 0.0, pltpu.roll(cur[0:1], 127, 2))
-            left = jnp.concatenate([left, cur[0:3]], axis=0)
-            right = jnp.concatenate([cur[1:4], right], axis=0)
+            edge_l = pltpu.roll(jnp.where(lane == 127, 0.0, cur[3:4]), 1, 2)
+            edge_r = pltpu.roll(jnp.where(lane == 0, 0.0, cur[0:1]), 127, 2)
+            left = jnp.concatenate([edge_l, cur[0:3]], axis=0)
+            right = jnp.concatenate([cur[1:4], edge_r], axis=0)
             beside = ((above + below) + (high + low)) + (left + right)
             w = quad(U[0, part(x + 1, t), :]) * cur - beside
             W[part(x + 1, t), :] = w.reshape(32, 128)
@@ -481,13 +481,15 @@
     copies = []
     for c in range(4):
         at = pl.ds(c * 128, 128)
-        copies.append(pltpu.make_async_copy(field.at[c], vel.at[:, at], sems.at[0, c]))
+        for h in range(4):
+            some = pl.ds(h * 256, 256)
+            copies.append(pltpu.make_async_copy(field.at[c, some], vel.at[some, at], sems.at[2 + h, c]))
         copies.append(pltpu.make_async_copy(lamx.at[pl.ds(c * 32, 32)], mx.at[:, at], sems.at[1, c]))
     for copy in copies:
         copy.start()
     for c in range(4):
         my_s[:, :, pl.ds(c * 128, 128)] = lamy[pl.ds(c * 32, 32), :].reshape(32, 1, 128)
-    copies.append(pltpu.make_async_copy(my_s, my, sems.at[2, 0]))
+    copies.append(pltpu.make_async_copy(my_s, my, sems.at[0, 0]))
     copies[-1].start()
     for copy in copies:
         copy.wait()
@@ -549,7 +551,7 @@
         ),
         in_specs=[vmem] * 3,
         out_specs=(hbm, hbm, hbm),
-        scratch_shapes=[pltpu.VMEM((32, 1, 512), F32), dma((3, 4))],
+        scratch_shapes=[pltpu.VMEM((32, 1, 512), F32), dma((6, 4))],
         compiler_params=pltpu.CompilerParams(vmem_limit_bytes=4 * 2**20),
         name="finish",
     )(xpre, lamx, lamy)

time: 65.2 us -> 65.2 us (level)
  no operation moved by 1% of the time
where the time goes in v8:
time: 65.2 us; the launch traced here: 65.1 us
  Pallas kernels  64.5 us (99%)
    pallas_call x1, Pallas kernels, on_device(): pl.pallas_call(functools.partial(kernel, ni, nj), out_shape=(pltpu.VMEM((...  62.9 us
    pallas_call x1, Pallas kernels, on_device(): pl.pallas_call(finish_kernel, out_shape=(jax.ShapeDtypeStruct((1024, 512)...  1.55 us

profile of v8, /device:TPU:1, one launch (start us, length us, event | category | flops | bytes accessed | tf_op | source)
XLA Modules:
  0.0 65.1 jit_solution(12676151289174850257)
XLA Ops:
  0.6 62.9 %solve.1 = (f32[4,1024,128]{2,1,0:T(8,128)S(1)}, f32[128,128]{1,0:T(8,128)S(1)}, f32[128,128]{1,0:T(8,128)S(1)}) custom-call(s32[1024,512]{1,0:T(8,128)} %bitcast.4, f32[8]{0:T(128)} %drag.1, f32[1024,512]{1,0:T(8,128)} %bitcast.5, f32[128,128]{1,0:T(8,128)} %cinv.1, s32[128]{0:T(128)} %owner.1), custom_call_target="tpu_custom_call" | custom-call | tf_op jit(solution)/shard_map/solve/pallas_call | solution.py:503
  63.5 1.6 %finish.1 = (f32[1024,512]{1,0:T(8,128)}, f32[32,512]{1,0:T(8,128)}, f32[32,1,512]{2,1,0:T(1,128)}) custom-call(f32[4,1024,128]{2,1,0:T(8,128)S(1)} %get-tuple-element.9.field, f32[128,128]{1,0:T(8,128)S(1)} %get-tuple-element.10.lamx, f32[128,128]{1,0:T(8,128)S(1)} %get-tuple-element.11.lamy), custom_call_target="tpu_custom_call" | custom-call | tf_op jit(solution)/shard_map/finish/pallas_call | solution.py:545
